TPU v7x, 32 devices: a whole 2x2x4 slice. The times are simulated.
32 devices in a mesh: cfg: 2 (over x), work: 16 (over z, y, core).
Axes of the slice: x: 2, y: 2, z: 4, core: 2. Of those that a mesh axis runs over, the one named last changes fastest.
Arguments:
- sources: bfloat16 [32, 16384, 128], P('cfg', 'work'), parts along dimension 0, may hold values from -6 to 6
- perambs: bfloat16 [192, 16384], P('cfg', 'work'), parts along dimension 0, may hold values from -0.5 to 0.5
- source_ids: int32 [16], replicated, may hold values from 0 to 15
- peramb_ids: int32 [48, 3], replicated, may hold values from 0 to 95
- sink_counts: int32 [16], replicated, may hold values from 1 to 6, 48 in all
- weights: float32 [48], replicated, may hold values from -2 to 2, as said below
Outputs:
- sink_tensors: bfloat16 [32, 16384, 128], P(('cfg', 'work')), parts along dimension 0
There are 2 independent parts, one for each index of `cfg`. A program takes and returns all parts, laid end to end along the dimension named above; an argument that names none is the same for every part. Nothing has to cross between parts.
Inputs may be any that keep to these rules, and one draw needn't show every extreme that they name: `sink_counts`: diagrams are listed sink by sink in order; the counts add up to 48 and some sink has exactly 6 diagrams. `weights`: nonzero multiples of 1/4.
All inputs are finite; a program needn't handle non-finite values.
Results may differ from a plain program's by a relative error of at most 0.0064.
Values may be sent and summed in bfloat16 or wider, within the bound.
No kernel may reach another device: no remote copies, remote signals or barrier semaphores. Data moves between devices by JAX's collectives and lax.ppermute only.
A program may use at most 128 MiB of HBM per device.

v0:
```python
import functools

import jax
import jax.numpy as jnp
from jax import lax
from jax.experimental import pallas as pl
from jax.experimental.pallas import tpu as pltpu
from jax.sharding import PartitionSpec as P

MOST = 6
LEGS = 3
UNIT_ROWS = 16
B_BLOCK = 16
GROUPS = ((0, 4), (1, 5), (2, 6), (3, 7))
VMEM = 56 * 1024 * 1024


def choose_kernel(
    workers, ids_ref, counts_ref, matrix_ids_ref, source_ref, peramb_ref, *refs
):
    piece_refs, matrix_ref = refs[:workers], refs[workers]
    sems, choice_ref, spread_ref = refs[workers + 1 :]
    own = lax.axis_index("work")
    copies = []
    for shift in range(workers):
        copy = pltpu.make_async_copy(
            source_ref.at[ids_ref[own ^ shift]], piece_refs[shift], sems.at[shift]
        )
        copy.start()
        copies.append(copy)

    rows = MOST * LEGS
    diagrams = matrix_ids_ref.shape[0]
    total = peramb_ref.shape[0]
    lanes = lax.broadcasted_iota(jnp.int32, (1, total), 1)

    def mark(sink, start):
        for slot in range(MOST):
            diagram = jnp.minimum(start + slot, diagrams - 1)
            for leg in range(LEGS):
                choice_ref[pl.ds(sink * rows + slot * LEGS + leg, 1), :] = jnp.where(
                    lanes == matrix_ids_ref[diagram, leg], 1.0, 0.0
                )
        return start + counts_ref[sink]

    lax.fori_loop(0, workers, mark, 0)
    chosen = jnp.dot(
        choice_ref[...].astype(jnp.bfloat16), peramb_ref[...], preferred_element_type=jnp.float32
    )
    extent = matrix_ref.shape[2]
    a_per = peramb_ref.shape[1] // extent
    for row in range(a_per):
        spread_ref[pl.ds(row, workers * rows, stride=a_per), :] = chosen[
            :, row * extent : (row + 1) * extent
        ]
    matrix_ref[...] = spread_ref[...].reshape(matrix_ref.shape).astype(jnp.bfloat16)
    for copy in copies:
        copy.wait()


def choose(sources, perambs, source_ids, peramb_ids, sink_counts, workers):
    extent = sources.shape[2]
    rows = MOST * LEGS
    a_per = perambs.shape[1] // extent
    smem = pl.BlockSpec(memory_space=pltpu.SMEM)
    anywhere = pl.BlockSpec(memory_space=pl.ANY)
    vmem = pl.BlockSpec(memory_space=pltpu.VMEM)
    outs = pl.pallas_call(
        functools.partial(choose_kernel, workers),
        in_specs=[smem, smem, smem, anywhere, vmem],
        out_specs=[anywhere] * workers + [vmem],
        out_shape=[jax.ShapeDtypeStruct(sources.shape[1:], sources.dtype)] * workers
        + [jax.ShapeDtypeStruct((workers, rows * a_per, extent), jnp.bfloat16)],
        scratch_shapes=[
            pltpu.SemaphoreType.DMA((workers,)),
            pltpu.VMEM((workers * rows, perambs.shape[0]), jnp.float32),
            pltpu.VMEM((workers * rows * a_per, extent), jnp.float32),
        ],
        compiler_params=pltpu.CompilerParams(vmem_limit_bytes=VMEM),
    )(source_ids, sink_counts, peramb_ids, sources, perambs)
    return outs[:workers], outs[workers]


def legs_kernel(
    workers, counts_ref, weights_ref, matrix_ref, leg3_ref, leg2_ref, leg1_ref, flat_ref, leg_ref
):
    extent = matrix_ref.shape[2]
    rows = MOST * LEGS
    a_per = matrix_ref.shape[1] // rows
    flat_ref[...] = matrix_ref[...].astype(jnp.float32).reshape(flat_ref.shape)
    own = lax.axis_index("work")
    start = lax.fori_loop(0, own, lambda i, total: total + counts_ref[i], 0)
    count = counts_ref[own]
    unit = UNIT_ROWS // a_per
    units = workers // unit
    for slot in range(MOST):
        for leg in range(LEGS):
            base = (slot * LEGS + leg) * a_per
            for row in range(a_per):
                leg_ref[pl.ds(row, workers, stride=a_per), :] = flat_ref[
                    pl.ds(base + row, workers, stride=rows * a_per), :
                ]
            if leg == 2:
                leg3_ref[:, slot * extent : (slot + 1) * extent] = leg_ref[...].T.astype(
                    jnp.bfloat16
                )
            elif leg == 1:
                leg2_ref[slot * extent : (slot + 1) * extent, :] = leg_ref[...].astype(
                    jnp.bfloat16
                )
            else:
                diagram = jnp.minimum(start + slot, weights_ref.shape[0] - 1)
                factor = jnp.where(slot < count, weights_ref[diagram], 0.0)
                leg_ref[...] = (factor * leg_ref[...]).T
                for block in range(units):
                    place = (own // unit) ^ block
                    leg1_ref[block, slot * UNIT_ROWS : (slot + 1) * UNIT_ROWS, :] = leg_ref[
                        pl.ds(pl.multiple_of(place * UNIT_ROWS, UNIT_ROWS), UNIT_ROWS), :
                    ].astype(jnp.bfloat16)


def make_legs(matrices, sink_counts, weights, workers):
    extent = matrices.shape[2]
    a_per = extent // workers
    smem = pl.BlockSpec(memory_space=pltpu.SMEM)
    vmem = pl.BlockSpec(memory_space=pltpu.VMEM)
    return pl.pallas_call(
        functools.partial(legs_kernel, workers),
        in_specs=[smem, smem, vmem],
        out_specs=[vmem] * 3,
        out_shape=[
            jax.ShapeDtypeStruct((extent, MOST * extent), jnp.bfloat16),
            jax.ShapeDtypeStruct((MOST * extent, extent), jnp.bfloat16),
            jax.ShapeDtypeStruct(
                (extent // UNIT_ROWS, MOST * UNIT_ROWS, extent), jnp.bfloat16
            ),
        ],
        scratch_shapes=[
            pltpu.VMEM((matrices.shape[0] * matrices.shape[1], extent), jnp.float32),
            pltpu.VMEM((extent, extent), jnp.float32),
        ],
        compiler_params=pltpu.CompilerParams(vmem_limit_bytes=VMEM),
    )(sink_counts, weights, matrices)


def group_kernel(first, last, units, per_unit, extent, *refs):
    pieces = len(units) * per_unit
    piece_refs = refs[:pieces]
    leg3_ref, leg2_ref, leg1_ref = refs[pieces : pieces + 3]
    refs = refs[pieces + 3 :]
    if not first:
        acc_ref, refs = refs[0], refs[1:]
    out_ref, turned_ref, outer_ref = refs[:3]
    a_per = piece_refs[0].shape[0] // extent
    unit_depth = MOST * UNIT_ROWS
    depth = unit_depth * len(units)
    pitch = depth + 8
    step = pl.program_id(0)

    def inner_legs(place, lane, piece_ref):
        sender = (lax.axis_index("work") & (per_unit - 1)) ^ lane
        third = jnp.dot(
            piece_ref[...], leg3_ref[...], preferred_element_type=jnp.float32
        ).astype(jnp.bfloat16)
        for d in range(MOST):
            columns = third[:, d * extent : (d + 1) * extent]
            wide = jnp.concatenate(
                [columns[a * extent : (a + 1) * extent] for a in range(a_per)], axis=1
            )
            second = jnp.dot(
                leg2_ref[d * extent : (d + 1) * extent, :],
                wide,
                preferred_element_type=jnp.float32,
            )
            for a in range(a_per):
                row = place * unit_depth + d * UNIT_ROWS + sender * a_per + a
                turned_ref[pl.ds(row, extent, stride=pitch), :] = second[
                    :, a * extent : (a + 1) * extent
                ]

    for piece in range(pieces):
        pl.when(step == piece)(
            functools.partial(
                inner_legs, piece // per_unit, piece % per_unit, piece_refs[piece]
            )
        )

    @pl.when(step == 0)
    def turn_outer():
        for place, unit in enumerate(units):
            outer_ref[place * unit_depth : (place + 1) * unit_depth, :] = leg1_ref[
                unit
            ].astype(jnp.float32)

    @pl.when(step >= pieces)
    def outer_leg():
        begin = (step - pieces) * B_BLOCK
        wide = jnp.concatenate(
            [
                turned_ref[pl.ds(pl.multiple_of((begin + b) * pitch, 8), depth), :].astype(
                    jnp.bfloat16
                )
                for b in range(B_BLOCK)
            ],
            axis=1,
        )
        outer = outer_ref[...].T.astype(jnp.bfloat16)
        whole = jnp.dot(outer, wide, preferred_element_type=jnp.float32)
        for b in range(B_BLOCK):
            part = whole[:, b * extent : (b + 1) * extent]
            if not first:
                part = part + acc_ref[b]
            if last:
                refs[3][pl.ds(b, extent, stride=B_BLOCK + 1), :] = part
            else:
                out_ref[b] = part
        if last:
            for a in range(extent):
                out_ref[a] = refs[3][pl.ds(a * (B_BLOCK + 1), B_BLOCK), :].astype(jnp.bfloat16)


def add_group(units, pieces, leg3, leg2, leg1, acc, last):
    extent = leg3.shape[0]
    count = len(pieces)
    per_unit = count // len(units)
    depth = MOST * UNIT_ROWS * len(units)
    first = acc is None
    blocks = extent // B_BLOCK

    def whole_spec(x):
        return pl.BlockSpec(x.shape, lambda i: (0,) * x.ndim)

    def block_of(i):
        return jnp.maximum(i - count, 0)

    operands = [*pieces, leg3, leg2, leg1]
    in_specs = [whole_spec(x) for x in operands]
    if not first:
        operands.append(acc)
        in_specs.append(pl.BlockSpec((B_BLOCK, extent, extent), lambda i: (block_of(i), 0, 0)))
    scratch = [
        pltpu.VMEM((extent * (depth + 8), extent), jnp.float32),
        pltpu.VMEM((depth, extent), jnp.float32),
    ]
    if last:
        out_shape = jax.ShapeDtypeStruct((extent, extent, extent), jnp.bfloat16)
        out_spec = pl.BlockSpec((extent, B_BLOCK, extent), lambda i: (0, block_of(i), 0))
        scratch.append(pltpu.VMEM((extent * (B_BLOCK + 1), extent), jnp.float32))
    else:
        out_shape = jax.ShapeDtypeStruct((extent, extent, extent), jnp.float32)
        out_spec = pl.BlockSpec((B_BLOCK, extent, extent), lambda i: (block_of(i), 0, 0))
    rows = count * pieces[0].shape[0]
    return pl.pallas_call(
        functools.partial(group_kernel, first, last, units, per_unit, extent),
        grid=(count + blocks,),
        in_specs=in_specs,
        out_specs=out_spec,
        out_shape=out_shape,
        scratch_shapes=scratch,
        compiler_params=pltpu.CompilerParams(
            dimension_semantics=("arbitrary",), vmem_limit_bytes=VMEM
        ),
        cost_estimate=pl.CostEstimate(
            flops=6 * MOST * rows * extent * extent,
            bytes_accessed=12 * extent**3,
            transcendentals=0,
        ),
    )(*operands)


def per_device(sources, perambs, source_ids, peramb_ids, sink_counts, weights):
    workers = lax.axis_size("work")
    extent = sources.shape[2]
    per_unit = UNIT_ROWS * workers // extent
    pieces, matrices = choose(sources, perambs, source_ids, peramb_ids, sink_counts, workers)
    matrices = lax.all_to_all(matrices, "work", split_axis=0, concat_axis=0, tiled=True)
    leg3, leg2, leg1 = make_legs(matrices, sink_counts, weights, workers)

    arrived = [pieces[0]]
    for shift in range(1, workers):
        arrived.append(
            lax.ppermute(pieces[shift], "work", [(i, i ^ shift) for i in range(workers)])
        )
    acc = None
    for group, units in enumerate(GROUPS):
        members = [arrived[u * per_unit + lane] for u in units for lane in range(per_unit)]
        acc = add_group(units, members, leg3, leg2, leg1, acc, group == len(GROUPS) - 1)
    return acc.reshape(1, extent * extent, extent)


def solution(mesh):
    return jax.shard_map(
        per_device,
        mesh=mesh,
        in_specs=(P("cfg", "work", None), P("cfg", "work"), P(), P(), P(), P()),
        out_specs=P(("cfg", "work"), None, None),
        check_vma=False,
    )
```

profile of v0, /device:TPU:11, one launch (start us, length us, event | category | flops | bytes accessed | tf_op | source)
XLA Modules:
  0.0 263.5 jit_solution(9834715459065492806)
XLA Ops:
  0.0 1.4 copy.7.matrix_ids_ref
  1.4 130.2 %shard_map.64 = (bf16[1024,128]{1,0:T(8,128)(2,1)}, bf16[1024,128]{1,0:T(8,128)(2,1)}, bf16[1024,128]{1,0:T(8,128)(2,1)}, bf16[1024,128]{1,0:T(8,128)(2,1)}, bf1...) custom-call(s32[16]{0:T(128)} %ids_ref.1, ...), custom_call_target="tpu_custom_call" | custom-call | tf_op jit(solution)/shard_map/pallas_call | solution.py:68
  131.6 6.8 %all-to-all-start = ((bf16[16,144,128]{2,1,0:T(8,128)(2,1)}), bf16[16,144,128]{2,1,0:T(8,128)(2,1)S(1)}, u32[]{:S(2)}, u32[]{:S(2)}) async-start(bf16[16,144,128]{2,1,0:T(8,128)(2,1)} %get-tuple-element.29), calls=%async_computation | async-start | bytes 1179648 | tf_op jit(solution)/shard_map/all_to_all | solution.py:276
  138.4 1.9 collective-permute-start.5
  140.3 1.2 collective-permute-start.6
  141.5 0.2 collective-permute-start.12
  141.7 1.1 collective-permute-start.13
  142.8 12.0 %collective-permute-done.4.refs_0_ = bf16[1024,128]{1,0:T(8,128)(2,1)S(1)} collective-permute-done((bf16[1024,128]{1,0:T(8,128)(2,1)}, bf16[1024,128]{1,0:T(8,128)(2,1)S(1)}, u32[]{:S(2)}, u32[]{:S(2)}) %collective-permute-start.4) | collective-permute-done | bytes 262176 | tf_op jit(solution)/shard_map/ppermute | solution.py:282
  154.9 3.1 %collective-permute-start.14 = (bf16[1024,128]{1,0:T(8,128)(2,1)}, bf16[1024,128]{1,0:T(8,128)(2,1)S(1)}, u32[]{:S(2)}, u32[]{:S(2)}) collective-permute-start(bf16[1024,128]{1,0:T(8,128)(2,1)} %get-tuple-element.44), channel_id=1, source_target_pairs={{0,9},{1,8},{2,11},{3,10},{4,13},{5,12},{6,15},{7,14},{8,1},{9,0},... | collective-permute-start | bytes 786440 | tf_op jit(solution)/shard_map/ppermute | solution.py:282
  158.0 10.4 %collective-permute-done.5.refs_1_ = bf16[1024,128]{1,0:T(8,128)(2,1)S(1)} collective-permute-done((bf16[1024,128]{1,0:T(8,128)(2,1)}, bf16[1024,128]{1,0:T(8,128)(2,1)S(1)}, u32[]{:S(2)}, u32[]{:S(2)}) %collective-permute-start.5) | collective-permute-done | bytes 262176 | tf_op jit(solution)/shard_map/ppermute | solution.py:282
  168.4 1.1 collective-permute-start.8
  169.5 1.5 collective-permute-start.9
  171.0 2.5 collective-permute-start.10
  173.6 11.6 %collective-permute-done.13.refs_2_ = bf16[1024,128]{1,0:T(8,128)(2,1)S(1)} collective-permute-done((bf16[1024,128]{1,0:T(8,128)(2,1)}, bf16[1024,128]{1,0:T(8,128)(2,1)S(1)}, u32[]{:S(2)}, u32[]{:S(2)}) %collective-permute-start.13) | collective-permute-done | bytes 262176 | tf_op jit(solution)/shard_map/ppermute | solution.py:282
  185.2 5.0 %collective-permute-start.11 = (bf16[1024,128]{1,0:T(8,128)(2,1)}, bf16[1024,128]{1,0:T(8,128)(2,1)S(1)}, u32[]{:S(2)}, u32[]{:S(2)}) collective-permute-start(bf16[1024,128]{1,0:T(8,128)(2,1)} %get-tuple-element.40), channel_id=1, source_target_pairs={{0,11},{1,10},{2,9},{3,8},{4,15},{5,14},{6,13},{7,12},{8,3},{9,2},... | collective-permute-start | bytes 786440 | tf_op jit(solution)/shard_map/ppermute | solution.py:282
  190.2 0.8 copy-done
  191.0 3.1 %shard_map.65 = (bf16[128,768]{1,0:T(8,128)(2,1)}, bf16[768,128]{1,0:T(8,128)(2,1)}, bf16[8,96,128]{2,1,0:T(8,128)(2,1)}) custom-call(s32[16]{0:T(128)} %counts_ref.3, f32[48]{0:T(128)} %weights_ref.1, bf16[16,144,128]{2,1,0:T(8,128)(2,1)} %copy-done), custom_call_target="tpu_custom_call" | custom-call | tf_op jit(solution)/shard_map/pallas_call | solution.py:127
  194.0 2.2 collective-permute-done.14.refs_3_
  196.2 2.5 collective-permute-start.7
  198.8 11.7 %shard_map.66.refs_7_ = f32[128,128,128]{2,1,0:T(8,128)} custom-call(bf16[1024,128]{1,0:T(8,128)(2,1)} %get-tuple-element.41.refs_0_, bf16[1024,128]{1,0:T(8,128)(2,1)} %copy-done.13, bf16[1024,128]{1,0:T(8,128)(2,1)} %copy-done.14, bf16[1024,128]{1,0:T(8,128)(2,1)} %copy-done.15, bf16[128,768]{1,0:T(8,128)(2,1)} %get-tuple-element.30.refs_4_, ...), custom_call_target="tpu_custom_call" | custom-call | flops 2415919104 | bytes 25165824 | tf_op jit(solution)/shard_map/pallas_call | solution.py:253
  210.5 3.2 %collective-permute-start = (bf16[1024,128]{1,0:T(8,128)(2,1)S(1)}, bf16[1024,128]{1,0:T(8,128)(2,1)S(1)}, u32[]{:S(2)}, u32[]{:S(2)}) collective-permute-start(bf16[1024,128]{1,0:T(8,128)(2,1)S(1)} %copy-done.19), channel_id=1, source_target_pairs={{0,6},{1,7},{2,4},{3,5},{4,2},{5,3},{6,0},{7,1},{8,14},{9,15},{10,... | collective-permute-start | bytes 786440 | tf_op jit(solution)/shard_map/ppermute | solution.py:282
  213.7 0.5 collective-permute-start.1
  214.2 1.3 collective-permute-start.2
  215.5 1.7 collective-permute-start.3
  217.2 14.8 %shard_map.67.refs_7_ = f32[128,128,128]{2,1,0:T(8,128)} custom-call(bf16[1024,128]{1,0:T(8,128)(2,1)} %copy-done.4, bf16[1024,128]{1,0:T(8,128)(2,1)} %copy-done.5, bf16[1024,128]{1,0:T(8,128)(2,1)} %copy-done.6, bf16[1024,128]{1,0:T(8,128)(2,1)} %copy-done.7, bf16[128,768]{1,0:T(8,128)(2,1)} %get-tuple-element.30.refs_4_, ...), custom_call_target="tpu_custom_call" | custom-call | flops 2415919104 | bytes 25165824 | tf_op jit(solution)/shard_map/pallas_call | solution.py:253
  232.1 0.7 copy-done.10
  232.8 14.9 %shard_map.68.refs_7_ = f32[128,128,128]{2,1,0:T(8,128)} custom-call(bf16[1024,128]{1,0:T(8,128)(2,1)} %copy-done.1, bf16[1024,128]{1,0:T(8,128)(2,1)} %copy-done.2, bf16[1024,128]{1,0:T(8,128)(2,1)} %copy-done.3, bf16[1024,128]{1,0:T(8,128)(2,1)} %copy-done.10, bf16[128,768]{1,0:T(8,128)(2,1)} %get-tuple-element.30.refs_4_, ...), custom_call_target="tpu_custom_call" | custom-call | flops 2415919104 | bytes 25165824 | tf_op jit(solution)/shard_map/pallas_call | solution.py:253
  247.7 0.7 copy-done.8
  248.4 0.1 copy-done.9
  248.5 0.1 copy-done.11
  248.6 0.7 copy-done.12
  249.3 14.2 %shard_map.69 = bf16[128,128,128]{2,1,0:T(8,128)(2,1)} custom-call(bf16[1024,128]{1,0:T(8,128)(2,1)} %copy-done.8, bf16[1024,128]{1,0:T(8,128)(2,1)} %copy-done.9, bf16[1024,128]{1,0:T(8,128)(2,1)} %copy-done.11, bf16[1024,128]{1,0:T(8,128)(2,1)} %copy-done.12, bf16[128,768]{1,0:T(8,128)(2,1)} %get-tuple-element.30.refs_4_, ...), custom_call_target="tpu_custom_call" | custom-call | flops 2415919104 | bytes 25165824 | tf_op jit(solution)/shard_map/pallas_call | solution.py:253
  (47 shorter events, 0.2 us)
Async XLA Ops:
  131.6 83.9 %copy-start.16 = (bf16[1024,128]{1,0:T(8,128)(2,1)S(1)}, bf16[1024,128]{1,0:T(8,128)(2,1)}, u32[]{:S(2)}) copy-start(bf16[1024,128]{1,0:T(8,128)(2,1)} %get-tuple-element.28) | copy-start | bytes 786436
  131.6 58.6 %all-to-all-start = ((bf16[16,144,128]{2,1,0:T(8,128)(2,1)}), bf16[16,144,128]{2,1,0:T(8,128)(2,1)S(1)}, u32[]{:S(2)}, u32[]{:S(2)}) async-start(bf16[16,144,128]{2,1,0:T(8,128)(2,1)} %get-tuple-element.29), calls=%async_computation | async-start | bytes 1179648 | tf_op jit(solution)/shard_map/all_to_all | solution.py:276
  138.3 16.5 %collective-permute-start.4 = (bf16[1024,128]{1,0:T(8,128)(2,1)}, bf16[1024,128]{1,0:T(8,128)(2,1)S(1)}, u32[]{:S(2)}, u32[]{:S(2)}) collective-permute-start(bf16[1024,128]{1,0:T(8,128)(2,1)} %get-tuple-element.33), channel_id=1, source_target_pairs={{0,4},{1,5},{2,6},{3,7},{4,0},{5,1},{6,2},{7,3},{8,12},{9,13},{10,... | collective-permute-start | bytes 786440 | tf_op jit(solution)/shard_map/ppermute | solution.py:282
  138.4 30.0 %collective-permute-start.5 = (bf16[1024,128]{1,0:T(8,128)(2,1)}, bf16[1024,128]{1,0:T(8,128)(2,1)S(1)}, u32[]{:S(2)}, u32[]{:S(2)}) collective-permute-start(bf16[1024,128]{1,0:T(8,128)(2,1)} %get-tuple-element.34), channel_id=1, source_target_pairs={{0,5},{1,4},{2,7},{3,6},{4,1},{5,0},{6,3},{7,2},{8,13},{9,12},{10,... | collective-permute-start | bytes 786440 | tf_op jit(solution)/shard_map/ppermute | solution.py:282
  140.3 29.2 %collective-permute-start.6 = (bf16[1024,128]{1,0:T(8,128)(2,1)}, bf16[1024,128]{1,0:T(8,128)(2,1)S(1)}, u32[]{:S(2)}, u32[]{:S(2)}) collective-permute-start(bf16[1024,128]{1,0:T(8,128)(2,1)} %get-tuple-element.35), channel_id=1, source_target_pairs={{0,12},{1,13},{2,14},{3,15},{4,8},{5,9},{6,10},{7,11},{8,4},{9,5},... | collective-permute-start | bytes 786440 | tf_op jit(solution)/shard_map/ppermute | solution.py:282
  141.5 29.5 %collective-permute-start.12 = (bf16[1024,128]{1,0:T(8,128)(2,1)}, bf16[1024,128]{1,0:T(8,128)(2,1)S(1)}, u32[]{:S(2)}, u32[]{:S(2)}) collective-permute-start(bf16[1024,128]{1,0:T(8,128)(2,1)} %get-tuple-element.42), channel_id=1, source_target_pairs={{0,1},{1,0},{2,3},{3,2},{4,5},{5,4},{6,7},{7,6},{8,9},{9,8},{10,11... | collective-permute-start | bytes 786440 | tf_op jit(solution)/shard_map/ppermute | solution.py:282
  141.7 43.5 %collective-permute-start.13 = (bf16[1024,128]{1,0:T(8,128)(2,1)}, bf16[1024,128]{1,0:T(8,128)(2,1)S(1)}, u32[]{:S(2)}, u32[]{:S(2)}) collective-permute-start(bf16[1024,128]{1,0:T(8,128)(2,1)} %get-tuple-element.43), channel_id=1, source_target_pairs={{0,8},{1,9},{2,10},{3,11},{4,12},{5,13},{6,14},{7,15},{8,0},{9,1},... | collective-permute-start | bytes 786440 | tf_op jit(solution)/shard_map/ppermute | solution.py:282
  154.9 77.2 %copy-start.1 = (bf16[1024,128]{1,0:T(8,128)(2,1)}, bf16[1024,128]{1,0:T(8,128)(2,1)S(1)}, u32[]{:S(2)}) copy-start(bf16[1024,128]{1,0:T(8,128)(2,1)S(1)} %collective-permute-done.4.refs_0_) | copy-start | bytes 786436
  154.9 41.4 %collective-permute-start.14 = (bf16[1024,128]{1,0:T(8,128)(2,1)}, bf16[1024,128]{1,0:T(8,128)(2,1)S(1)}, u32[]{:S(2)}, u32[]{:S(2)}) collective-permute-start(bf16[1024,128]{1,0:T(8,128)(2,1)} %get-tuple-element.44), channel_id=1, source_target_pairs={{0,9},{1,8},{2,11},{3,10},{4,13},{5,12},{6,15},{7,14},{8,1},{9,0},... | collective-permute-start | bytes 786440 | tf_op jit(solution)/shard_map/ppermute | solution.py:282
  168.4 63.7 %copy-start.2 = (bf16[1024,128]{1,0:T(8,128)(2,1)}, bf16[1024,128]{1,0:T(8,128)(2,1)S(1)}, u32[]{:S(2)}) copy-start(bf16[1024,128]{1,0:T(8,128)(2,1)S(1)} %collective-permute-done.5.refs_1_) | copy-start | bytes 786436
  168.4 42.1 %collective-permute-start.8 = (bf16[1024,128]{1,0:T(8,128)(2,1)}, bf16[1024,128]{1,0:T(8,128)(2,1)S(1)}, u32[]{:S(2)}, u32[]{:S(2)}) collective-permute-start(bf16[1024,128]{1,0:T(8,128)(2,1)} %get-tuple-element.37), channel_id=1, source_target_pairs={{0,2},{1,3},{2,0},{3,1},{4,6},{5,7},{6,4},{7,5},{8,10},{9,11},{10,... | collective-permute-start | bytes 786440 | tf_op jit(solution)/shard_map/ppermute | solution.py:282
  169.5 62.6 %copy-start.3 = (bf16[1024,128]{1,0:T(8,128)(2,1)}, bf16[1024,128]{1,0:T(8,128)(2,1)S(1)}, u32[]{:S(2)}) copy-start(bf16[1024,128]{1,0:T(8,128)(2,1)S(1)} %collective-permute-done.6.refs_2_) | copy-start | bytes 786436
  169.5 44.2 %collective-permute-start.9 = (bf16[1024,128]{1,0:T(8,128)(2,1)}, bf16[1024,128]{1,0:T(8,128)(2,1)S(1)}, u32[]{:S(2)}, u32[]{:S(2)}) collective-permute-start(bf16[1024,128]{1,0:T(8,128)(2,1)} %get-tuple-element.38), channel_id=1, source_target_pairs={{0,3},{1,2},{2,1},{3,0},{4,7},{5,6},{6,5},{7,4},{8,11},{9,10},{10,... | collective-permute-start | bytes 786440 | tf_op jit(solution)/shard_map/ppermute | solution.py:282
  171.0 27.7 %copy-start.13 = (bf16[1024,128]{1,0:T(8,128)(2,1)}, bf16[1024,128]{1,0:T(8,128)(2,1)S(1)}, u32[]{:S(2)}) copy-start(bf16[1024,128]{1,0:T(8,128)(2,1)S(1)} %collective-permute-done.12.refs_1_) | copy-start | bytes 786436
  171.0 43.1 %collective-permute-start.10 = (bf16[1024,128]{1,0:T(8,128)(2,1)}, bf16[1024,128]{1,0:T(8,128)(2,1)S(1)}, u32[]{:S(2)}, u32[]{:S(2)}) collective-permute-start(bf16[1024,128]{1,0:T(8,128)(2,1)} %get-tuple-element.39), channel_id=1, source_target_pairs={{0,10},{1,11},{2,8},{3,9},{4,14},{5,15},{6,12},{7,13},{8,2},{9,3},... | collective-permute-start | bytes 786440 | tf_op jit(solution)/shard_map/ppermute | solution.py:282
  185.2 13.6 %copy-start.14 = (bf16[1024,128]{1,0:T(8,128)(2,1)}, bf16[1024,128]{1,0:T(8,128)(2,1)S(1)}, u32[]{:S(2)}) copy-start(bf16[1024,128]{1,0:T(8,128)(2,1)S(1)} %collective-permute-done.13.refs_2_) | copy-start | bytes 786436
  185.2 30.4 %collective-permute-start.11 = (bf16[1024,128]{1,0:T(8,128)(2,1)}, bf16[1024,128]{1,0:T(8,128)(2,1)S(1)}, u32[]{:S(2)}, u32[]{:S(2)}) collective-permute-start(bf16[1024,128]{1,0:T(8,128)(2,1)} %get-tuple-element.40), channel_id=1, source_target_pairs={{0,11},{1,10},{2,9},{3,8},{4,15},{5,14},{6,13},{7,12},{8,3},{9,2},... | collective-permute-start | bytes 786440 | tf_op jit(solution)/shard_map/ppermute | solution.py:282
  191.0 19.5 %copy-start.19 = (bf16[1024,128]{1,0:T(8,128)(2,1)S(1)}, bf16[1024,128]{1,0:T(8,128)(2,1)}, u32[]{:S(2)}) copy-start(bf16[1024,128]{1,0:T(8,128)(2,1)} %get-tuple-element.25) | copy-start | bytes 786436
  191.0 22.7 %copy-start.18 = (bf16[1024,128]{1,0:T(8,128)(2,1)S(1)}, bf16[1024,128]{1,0:T(8,128)(2,1)}, u32[]{:S(2)}) copy-start(bf16[1024,128]{1,0:T(8,128)(2,1)} %get-tuple-element.26) | copy-start | bytes 786436
  191.0 23.2 %copy-start.17 = (bf16[1024,128]{1,0:T(8,128)(2,1)S(1)}, bf16[1024,128]{1,0:T(8,128)(2,1)}, u32[]{:S(2)}) copy-start(bf16[1024,128]{1,0:T(8,128)(2,1)} %get-tuple-element.27) | copy-start | bytes 786436
  196.2 2.5 copy-start.15
  196.2 35.8 %collective-permute-start.7 = (bf16[1024,128]{1,0:T(8,128)(2,1)}, bf16[1024,128]{1,0:T(8,128)(2,1)S(1)}, u32[]{:S(2)}, u32[]{:S(2)}) collective-permute-start(bf16[1024,128]{1,0:T(8,128)(2,1)} %get-tuple-element.36), channel_id=1, source_target_pairs={{0,13},{1,12},{2,15},{3,14},{4,9},{5,8},{6,11},{7,10},{8,5},{9,4},... | collective-permute-start | bytes 786440 | tf_op jit(solution)/shard_map/ppermute | solution.py:282
  210.5 6.7 %copy-start.4 = (bf16[1024,128]{1,0:T(8,128)(2,1)}, bf16[1024,128]{1,0:T(8,128)(2,1)S(1)}, u32[]{:S(2)}) copy-start(bf16[1024,128]{1,0:T(8,128)(2,1)S(1)} %collective-permute-done.8.refs_0_) | copy-start | bytes 786436
  210.5 37.2 %collective-permute-start = (bf16[1024,128]{1,0:T(8,128)(2,1)S(1)}, bf16[1024,128]{1,0:T(8,128)(2,1)S(1)}, u32[]{:S(2)}, u32[]{:S(2)}) collective-permute-start(bf16[1024,128]{1,0:T(8,128)(2,1)S(1)} %copy-done.19), channel_id=1, source_target_pairs={{0,6},{1,7},{2,4},{3,5},{4,2},{5,3},{6,0},{7,1},{8,14},{9,15},{10,... | collective-permute-start | bytes 786440 | tf_op jit(solution)/shard_map/ppermute | solution.py:282
  213.7 3.5 %copy-start.5 = (bf16[1024,128]{1,0:T(8,128)(2,1)}, bf16[1024,128]{1,0:T(8,128)(2,1)S(1)}, u32[]{:S(2)}) copy-start(bf16[1024,128]{1,0:T(8,128)(2,1)S(1)} %collective-permute-done.9.refs_1_) | copy-start | bytes 786436
  213.7 34.0 %collective-permute-start.1 = (bf16[1024,128]{1,0:T(8,128)(2,1)S(1)}, bf16[1024,128]{1,0:T(8,128)(2,1)S(1)}, u32[]{:S(2)}, u32[]{:S(2)}) collective-permute-start(bf16[1024,128]{1,0:T(8,128)(2,1)S(1)} %copy-done.18), channel_id=1, source_target_pairs={{0,7},{1,6},{2,5},{3,4},{4,3},{5,2},{6,1},{7,0},{8,15},{9,14},{10,... | collective-permute-start | bytes 786440 | tf_op jit(solution)/shard_map/ppermute | solution.py:282
  214.2 3.1 %copy-start.6 = (bf16[1024,128]{1,0:T(8,128)(2,1)}, bf16[1024,128]{1,0:T(8,128)(2,1)S(1)}, u32[]{:S(2)}) copy-start(bf16[1024,128]{1,0:T(8,128)(2,1)S(1)} %collective-permute-done.10.refs_2_) | copy-start | bytes 786436
  214.2 33.5 %collective-permute-start.2 = (bf16[1024,128]{1,0:T(8,128)(2,1)S(1)}, bf16[1024,128]{1,0:T(8,128)(2,1)S(1)}, u32[]{:S(2)}, u32[]{:S(2)}) collective-permute-start(bf16[1024,128]{1,0:T(8,128)(2,1)S(1)} %copy-done.17), channel_id=1, source_target_pairs={{0,14},{1,15},{2,12},{3,13},{4,10},{5,11},{6,8},{7,9},{8,6},{9,7},... | collective-permute-start | bytes 786440 | tf_op jit(solution)/shard_map/ppermute | solution.py:282
  215.5 1.7 copy-start.7
  215.5 32.2 %collective-permute-start.3 = (bf16[1024,128]{1,0:T(8,128)(2,1)S(1)}, bf16[1024,128]{1,0:T(8,128)(2,1)S(1)}, u32[]{:S(2)}, u32[]{:S(2)}) collective-permute-start(bf16[1024,128]{1,0:T(8,128)(2,1)S(1)} %copy-done.16), channel_id=1, source_target_pairs={{0,15},{1,14},{2,13},{3,12},{4,11},{5,10},{6,9},{7,8},{8,7},{9,6},... | collective-permute-start | bytes 786440 | tf_op jit(solution)/shard_map/ppermute | solution.py:282
  247.7 0.8 copy-start.9
  247.7 0.9 copy-start.11
  (4 other events, 2.9 us)
where the time goes:
time: 269 us; the launch traced here: 264 us
  Pallas kernels  189 us (70%)
  waiting for transfers between devices  36.3 us (13%)
  starting transfers between devices  33.7 us (13%)
  local copies, waits for them, and re-layouts  4.51 us (2%)
    pallas_call x1, Pallas kernels, choose(): pl.pallas_call(functools.partial(choose_kernel, workers), in_specs=[smem,...  130 us
    pallas_call x4, Pallas kernels, add_group(): pl.pallas_call(functools.partial(group_kernel, first, last, units, per_un...  55.6 us
    ppermute x15, waiting for transfers between devices, per_device(): lax.ppermute(pieces[shift], 'work', [(i, i ^ shift) for i in range(worker...  36.3 us
    ppermute x15, starting transfers between devices, per_device(): lax.ppermute(pieces[shift], 'work', [(i, i ^ shift) for i in range(worker...  27 us
    all_to_all x1, starting transfers between devices, per_device(): lax.all_to_all(matrices, 'work', split_axis=0, concat_axis=0, tiled=True)  6.75 us
  transfers between devices with their start and end apart: 16, of which 4 were waited for; matrix products, arithmetic and copies ran while one was open for 0% of the time, Pallas kernels for 17%

commit v1 on v0

--- a/solution.py
+++ b/solution.py
@@ -10,25 +10,40 @@
 MOST = 6
 LEGS = 3
 UNIT_ROWS = 16
-B_BLOCK = 16
-GROUPS = ((0, 4), (1, 5), (2, 6), (3, 7))
+B_BLOCK = 64
+ACC = jnp.bfloat16
+SENT = (4, 0, 1, 5, 2, 3, 6, 7)
+GROUPS = ((0, 1, 2, 4, 5), (3, 6), (7,))
+IN_FLIGHT = 5
 VMEM = 56 * 1024 * 1024
 
 
-def choose_kernel(
-    workers, ids_ref, counts_ref, matrix_ids_ref, source_ref, peramb_ref, *refs
-):
-    piece_refs, matrix_ref = refs[:workers], refs[workers]
-    sems, choice_ref, spread_ref = refs[workers + 1 :]
+def pieces_kernel(shifts, ids_ref, source_ref, *refs):
+    piece_refs, sems = refs[: len(shifts)], refs[len(shifts)]
     own = lax.axis_index("work")
     copies = []
-    for shift in range(workers):
+    for i, shift in enumerate(shifts):
         copy = pltpu.make_async_copy(
-            source_ref.at[ids_ref[own ^ shift]], piece_refs[shift], sems.at[shift]
+            source_ref.at[ids_ref[own ^ shift]], piece_refs[i], sems.at[i]
         )
         copy.start()
         copies.append(copy)
-
+    for copy in copies:
+        copy.wait()
+
+
+def choose_pieces(sources, source_ids, shifts):
+    return pl.pallas_call(
+        functools.partial(pieces_kernel, shifts),
+        in_specs=[pl.BlockSpec(memory_space=pltpu.SMEM), pl.BlockSpec(memory_space=pl.ANY)],
+        out_specs=[pl.BlockSpec(memory_space=pltpu.VMEM)] * len(shifts),
+        out_shape=[jax.ShapeDtypeStruct(sources.shape[1:], sources.dtype)] * len(shifts),
+        scratch_shapes=[pltpu.SemaphoreType.DMA((len(shifts),))],
+        compiler_params=pltpu.CompilerParams(vmem_limit_bytes=VMEM),
+    )(source_ids, sources)
+
+
+def matrices_kernel(workers, counts_ref, matrix_ids_ref, peramb_ref, matrix_ref, choice_ref, spread_ref):
     rows = MOST * LEGS
     diagrams = matrix_ids_ref.shape[0]
     total = peramb_ref.shape[0]
@@ -54,31 +69,24 @@
             :, row * extent : (row + 1) * extent
         ]
     matrix_ref[...] = spread_ref[...].reshape(matrix_ref.shape).astype(jnp.bfloat16)
-    for copy in copies:
-        copy.wait()
-
-
-def choose(sources, perambs, source_ids, peramb_ids, sink_counts, workers):
-    extent = sources.shape[2]
+
+
+def choose_matrices(perambs, peramb_ids, sink_counts, workers, extent):
     rows = MOST * LEGS
     a_per = perambs.shape[1] // extent
     smem = pl.BlockSpec(memory_space=pltpu.SMEM)
-    anywhere = pl.BlockSpec(memory_space=pl.ANY)
     vmem = pl.BlockSpec(memory_space=pltpu.VMEM)
-    outs = pl.pallas_call(
-        functools.partial(choose_kernel, workers),
-        in_specs=[smem, smem, smem, anywhere, vmem],
-        out_specs=[anywhere] * workers + [vmem],
-        out_shape=[jax.ShapeDtypeStruct(sources.shape[1:], sources.dtype)] * workers
-        + [jax.ShapeDtypeStruct((workers, rows * a_per, extent), jnp.bfloat16)],
+    return pl.pallas_call(
+        functools.partial(matrices_kernel, workers),
+        in_specs=[smem, smem, vmem],
+        out_specs=vmem,
+        out_shape=jax.ShapeDtypeStruct((workers, rows * a_per, extent), jnp.bfloat16),
         scratch_shapes=[
-            pltpu.SemaphoreType.DMA((workers,)),
             pltpu.VMEM((workers * rows, perambs.shape[0]), jnp.float32),
             pltpu.VMEM((workers * rows * a_per, extent), jnp.float32),
         ],
         compiler_params=pltpu.CompilerParams(vmem_limit_bytes=VMEM),
-    )(source_ids, sink_counts, peramb_ids, sources, perambs)
-    return outs[:workers], outs[workers]
+    )(sink_counts, peramb_ids, perambs)
 
 
 def legs_kernel(
@@ -150,7 +158,7 @@
     refs = refs[pieces + 3 :]
     if not first:
         acc_ref, refs = refs[0], refs[1:]
-    out_ref, turned_ref, outer_ref = refs[:3]
+    out_ref, turned_ref, outer_ref, across_ref = refs[:4]
     a_per = piece_refs[0].shape[0] // extent
     unit_depth = MOST * UNIT_ROWS
     depth = unit_depth * len(units)
@@ -191,6 +199,7 @@
             outer_ref[place * unit_depth : (place + 1) * unit_depth, :] = leg1_ref[
                 unit
             ].astype(jnp.float32)
+        across_ref[...] = outer_ref[...].T.astype(jnp.bfloat16)
 
     @pl.when(step >= pieces)
     def outer_leg():
@@ -204,19 +213,18 @@
             ],
             axis=1,
         )
-        outer = outer_ref[...].T.astype(jnp.bfloat16)
-        whole = jnp.dot(outer, wide, preferred_element_type=jnp.float32)
+        whole = jnp.dot(across_ref[...], wide, preferred_element_type=jnp.float32)
         for b in range(B_BLOCK):
             part = whole[:, b * extent : (b + 1) * extent]
             if not first:
-                part = part + acc_ref[b]
+                part = part + acc_ref[b].astype(jnp.float32)
             if last:
-                refs[3][pl.ds(b, extent, stride=B_BLOCK + 1), :] = part
+                refs[4][pl.ds(b, extent, stride=B_BLOCK + 8), :] = part
             else:
-                out_ref[b] = part
+                out_ref[b] = part.astype(out_ref.dtype)
         if last:
             for a in range(extent):
-                out_ref[a] = refs[3][pl.ds(a * (B_BLOCK + 1), B_BLOCK), :].astype(jnp.bfloat16)
+                out_ref[a] = refs[4][pl.ds(a * (B_BLOCK + 8), B_BLOCK), :].astype(jnp.bfloat16)
 
 
 def add_group(units, pieces, leg3, leg2, leg1, acc, last):
@@ -241,13 +249,14 @@
     scratch = [
         pltpu.VMEM((extent * (depth + 8), extent), jnp.float32),
         pltpu.VMEM((depth, extent), jnp.float32),
+        pltpu.VMEM((extent, depth), jnp.bfloat16),
     ]
     if last:
         out_shape = jax.ShapeDtypeStruct((extent, extent, extent), jnp.bfloat16)
         out_spec = pl.BlockSpec((extent, B_BLOCK, extent), lambda i: (0, block_of(i), 0))
-        scratch.append(pltpu.VMEM((extent * (B_BLOCK + 1), extent), jnp.float32))
+        scratch.append(pltpu.VMEM((extent * (B_BLOCK + 8), extent), jnp.float32))
     else:
-        out_shape = jax.ShapeDtypeStruct((extent, extent, extent), jnp.float32)
+        out_shape = jax.ShapeDtypeStruct((extent, extent, extent), ACC)
         out_spec = pl.BlockSpec((B_BLOCK, extent, extent), lambda i: (block_of(i), 0, 0))
     rows = count * pieces[0].shape[0]
     return pl.pallas_call(
@@ -272,15 +281,22 @@
     workers = lax.axis_size("work")
     extent = sources.shape[2]
     per_unit = UNIT_ROWS * workers // extent
-    pieces, matrices = choose(sources, perambs, source_ids, peramb_ids, sink_counts, workers)
+    order = [u * per_unit + lane for u in SENT for lane in range(per_unit)]
+    order.remove(0)
+    early, late = tuple(order[:IN_FLIGHT]), (0, *order[IN_FLIGHT:])
+    pieces = dict(zip(early, choose_pieces(sources, source_ids, early)))
+    pieces.update(zip(late, choose_pieces(sources, source_ids, late)))
+    matrices = choose_matrices(perambs, peramb_ids, sink_counts, workers, extent)
     matrices = lax.all_to_all(matrices, "work", split_axis=0, concat_axis=0, tiled=True)
     leg3, leg2, leg1 = make_legs(matrices, sink_counts, weights, workers)
 
-    arrived = [pieces[0]]
-    for shift in range(1, workers):
-        arrived.append(
-            lax.ppermute(pieces[shift], "work", [(i, i ^ shift) for i in range(workers)])
-        )
+    arrived = {0: pieces[0]}
+    for place, shift in enumerate(order):
+        piece = pieces[shift]
+        if place >= IN_FLIGHT:
+            before = order[place - IN_FLIGHT]
+            piece, arrived[before] = lax.optimization_barrier((piece, arrived[before]))
+        arrived[shift] = lax.ppermute(piece, "work", [(i, i ^ shift) for i in range(workers)])
     acc = None
     for group, units in enumerate(GROUPS):
         members = [arrived[u * per_unit + lane] for u in units for lane in range(per_unit)]

time: 269 us -> 138 us (0.51)
  the two profiles are of different devices: /device:TPU:11 before, /device:TPU:5 now
where the time goes in v1:
time: 138 us; the launch traced here: 137 us
  waiting for transfers between devices  54.1 us (39%)
  Pallas kernels  49 us (36%)
  starting transfers between devices  26.2 us (19%)
  local copies, waits for them, and re-layouts  7.89 us (6%)
    ppermute x15, waiting for transfers between devices, per_device(): lax.ppermute(piece, 'work', [(i, i ^ shift) for i in range(workers)])  54.1 us
    pallas_call x3, Pallas kernels, add_group(): pl.pallas_call(functools.partial(group_kernel, first, last, units, per_un...  36.1 us
    ppermute x15, starting transfers between devices, per_device(): lax.ppermute(piece, 'work', [(i, i ^ shift) for i in range(workers)])  19.5 us
    unnamed x33, local copies, waits for them, and re-layouts  7.89 us
    pallas_call x2, Pallas kernels, choose_pieces(): pl.pallas_call(functools.partial(pieces_kernel, shifts), in_specs=[pl.Blo...  7.21 us
    all_to_all x1, starting transfers between devices, per_device(): lax.all_to_all(matrices, 'work', split_axis=0, concat_axis=0, tiled=True)  6.67 us
    pallas_call x1, Pallas kernels, make_legs(): pl.pallas_call(functools.partial(legs_kernel, workers), in_specs=[smem, s...  3.01 us
  transfers between devices with their start and end apart: 16, of which 5 were waited for; matrix products, arithmetic and copies ran while one was open for 0% of the time, Pallas kernels for 28%

profile of v1, /device:TPU:5, one launch (start us, length us, event | category | flops | bytes accessed | tf_op | source)
XLA Modules:
  0.0 137.3 jit_solution(119916046036703636)
XLA Ops:
  0.0 1.4 copy.7.matrix_ids_ref
  1.4 2.6 %shard_map.66 = bf16[16,144,128]{2,1,0:T(8,128)(2,1)} custom-call(s32[16]{0:T(128)} %counts_ref.3, s32[48,3]{1,0:T(8,128)} %copy.7.matrix_ids_ref, bf16[96,1024]{1,0:T(8,128)(2,1)} %peramb_ref.1), custom_call_target="tpu_custom_call" | custom-call | tf_op jit(solution)/shard_map/pallas_call | solution.py:79
  4.0 6.7 %all-to-all-start = ((bf16[16,144,128]{2,1,0:T(8,128)(2,1)}), bf16[16,144,128]{2,1,0:T(8,128)(2,1)S(1)}, u32[]{:S(2)}, u32[]{:S(2)}) async-start(bf16[16,144,128]{2,1,0:T(8,128)(2,1)} %shard_map.66), calls=%async_computation | async-start | bytes 1179648 | tf_op jit(solution)/shard_map/all_to_all | solution.py:290
  10.6 3.1 %shard_map.65 = (bf16[1024,128]{1,0:T(8,128)(2,1)}, bf16[1024,128]{1,0:T(8,128)(2,1)}, bf16[1024,128]{1,0:T(8,128)(2,1)}, bf16[1024,128]{1,0:T(8,128)(2,1)}, bf16[1024,128]{1,0:T(8,128)(2,1)}) custom-call(s32[16]{0:T(128)} %ids_ref.3, bf16[16,1024,128]{2,1,0:T(8,128)(2,1)} %source_ref.3), custom_call_target="tpu_custom_call" | custom-call | tf_op jit(solution)/shard_map/pallas_call | solution.py:36
  14.2 2.1 %collective-permute-start.9 = (bf16[1024,128]{1,0:T(8,128)(2,1)}, bf16[1024,128]{1,0:T(8,128)(2,1)S(1)}, u32[]{:S(2)}, u32[]{:S(2)}) collective-permute-start(bf16[1024,128]{1,0:T(8,128)(2,1)} %get-tuple-element.65), channel_id=1, source_target_pairs={{0,9},{1,8},{2,11},{3,10},{4,13},{5,12},{6,15},{7,14},{8,1},{9,0},... | collective-permute-start | bytes 786440 | tf_op jit(solution)/shard_map/ppermute | solution.py:299
  16.9 1.6 %collective-permute-start = (bf16[1024,128]{1,0:T(8,128)(2,1)}, bf16[1024,128]{1,0:T(8,128)(2,1)S(1)}, u32[]{:S(2)}, u32[]{:S(2)}) collective-permute-start(bf16[1024,128]{1,0:T(8,128)(2,1)} %get-tuple-element.46), channel_id=1, source_target_pairs={{0,2},{1,3},{2,0},{3,1},{4,6},{5,7},{6,4},{7,5},{8,10},{9,11},{10,... | collective-permute-start | bytes 786440 | tf_op jit(solution)/shard_map/ppermute | solution.py:299
  18.6 4.1 %shard_map.64 = (bf16[1024,128]{1,0:T(8,128)(2,1)}, bf16[1024,128]{1,0:T(8,128)(2,1)}, bf16[1024,128]{1,0:T(8,128)(2,1)}, bf16[1024,128]{1,0:T(8,128)(2,1)}, bf1...) custom-call(s32[16]{0:T(128)} %ids_ref.3, ...), custom_call_target="tpu_custom_call" | custom-call | tf_op jit(solution)/shard_map/pallas_call | solution.py:36
  22.7 1.2 collective-permute-start.13
  23.9 20.0 %collective-permute-done.9.refs_7_ = bf16[1024,128]{1,0:T(8,128)(2,1)S(1)} collective-permute-done((bf16[1024,128]{1,0:T(8,128)(2,1)}, bf16[1024,128]{1,0:T(8,128)(2,1)S(1)}, u32[]{:S(2)}, u32[]{:S(2)}) %collective-permute-start.9) | collective-permute-done | bytes 262176 | tf_op jit(solution)/shard_map/ppermute | solution.py:299
  43.9 10.6 %collective-permute-done.6.refs_6_ = bf16[1024,128]{1,0:T(8,128)(2,1)S(1)} collective-permute-done((bf16[1024,128]{1,0:T(8,128)(2,1)}, bf16[1024,128]{1,0:T(8,128)(2,1)S(1)}, u32[]{:S(2)}, u32[]{:S(2)}) %collective-permute-start.6) | collective-permute-done | bytes 262176 | tf_op jit(solution)/shard_map/ppermute | solution.py:299
  54.5 2.4 %collective-permute-start.4 = (bf16[1024,128]{1,0:T(8,128)(2,1)}, bf16[1024,128]{1,0:T(8,128)(2,1)S(1)}, u32[]{:S(2)}, u32[]{:S(2)}) collective-permute-start(bf16[1024,128]{1,0:T(8,128)(2,1)} %get-tuple-element.52), channel_id=1, source_target_pairs={{0,6},{1,7},{2,4},{3,5},{4,2},{5,3},{6,0},{7,1},{8,14},{9,15},{10,... | collective-permute-start | bytes 786440 | tf_op jit(solution)/shard_map/ppermute | solution.py:299
  56.8 1.2 collective-permute-start.1
  58.0 0.7 copy-done.12
  58.7 2.8 %collective-permute-start.14 = (bf16[1024,128]{1,0:T(8,128)(2,1)}, bf16[1024,128]{1,0:T(8,128)(2,1)S(1)}, u32[]{:S(2)}, u32[]{:S(2)}) collective-permute-start(bf16[1024,128]{1,0:T(8,128)(2,1)} %get-tuple-element.72), channel_id=1, source_target_pairs={{0,13},{1,12},{2,15},{3,14},{4,9},{5,8},{6,11},{7,10},{8,5},{9,4},... | collective-permute-start | bytes 786440 | tf_op jit(solution)/shard_map/ppermute | solution.py:299
  61.5 5.0 %collective-permute-done.10.refs_9_ = bf16[1024,128]{1,0:T(8,128)(2,1)S(1)} collective-permute-done((bf16[1024,128]{1,0:T(8,128)(2,1)}, bf16[1024,128]{1,0:T(8,128)(2,1)S(1)}, u32[]{:S(2)}, u32[]{:S(2)}) %collective-permute-start.10) | collective-permute-done | bytes 262176 | tf_op jit(solution)/shard_map/ppermute | solution.py:299
  66.5 0.7 copy-done.13
  67.2 1.2 collective-permute-start.11
  68.3 3.0 %collective-permute-done.7.refs_8_ = bf16[1024,128]{1,0:T(8,128)(2,1)S(1)} collective-permute-done((bf16[1024,128]{1,0:T(8,128)(2,1)}, bf16[1024,128]{1,0:T(8,128)(2,1)S(1)}, u32[]{:S(2)}, u32[]{:S(2)}) %collective-permute-start.7) | collective-permute-done | bytes 262176 | tf_op jit(solution)/shard_map/ppermute | solution.py:299
  71.4 0.7 copy-done.14
  72.1 3.8 %collective-permute-start.5 = (bf16[1024,128]{1,0:T(8,128)(2,1)}, bf16[1024,128]{1,0:T(8,128)(2,1)S(1)}, u32[]{:S(2)}, u32[]{:S(2)}) collective-permute-start(bf16[1024,128]{1,0:T(8,128)(2,1)} %get-tuple-element.53), channel_id=1, source_target_pairs={{0,15},{1,14},{2,13},{3,12},{4,11},{5,10},{6,9},{7,8},{8,7},{9,6},... | collective-permute-start | bytes 786440 | tf_op jit(solution)/shard_map/ppermute | solution.py:299
  75.9 15.5 %collective-permute-done.1.refs_5_ = bf16[1024,128]{1,0:T(8,128)(2,1)S(1)} collective-permute-done((bf16[1024,128]{1,0:T(8,128)(2,1)}, bf16[1024,128]{1,0:T(8,128)(2,1)S(1)}, u32[]{:S(2)}, u32[]{:S(2)}) %collective-permute-start.1) | collective-permute-done | bytes 262176 | tf_op jit(solution)/shard_map/ppermute | solution.py:299
  91.4 0.7 copy-done.15
  92.1 2.2 %collective-permute-start.2 = (bf16[1024,128]{1,0:T(8,128)(2,1)}, bf16[1024,128]{1,0:T(8,128)(2,1)S(1)}, u32[]{:S(2)}, u32[]{:S(2)}) collective-permute-start(bf16[1024,128]{1,0:T(8,128)(2,1)} %get-tuple-element.48), channel_id=1, source_target_pairs={{0,14},{1,15},{2,12},{3,13},{4,10},{5,11},{6,8},{7,9},{8,6},{9,7},... | collective-permute-start | bytes 786440 | tf_op jit(solution)/shard_map/ppermute | solution.py:299
  94.3 0.8 copy-done
  95.1 3.0 %shard_map.67 = (bf16[128,768]{1,0:T(8,128)(2,1)}, bf16[768,128]{1,0:T(8,128)(2,1)}, bf16[8,96,128]{2,1,0:T(8,128)(2,1)}) custom-call(s32[16]{0:T(128)} %counts_ref.3, f32[48]{0:T(128)} %weights_ref.1, bf16[16,144,128]{2,1,0:T(8,128)(2,1)} %copy-done), custom_call_target="tpu_custom_call" | custom-call | tf_op jit(solution)/shard_map/pallas_call | solution.py:135
  98.2 17.7 %shard_map.68.refs_7_ = bf16[128,128,128]{2,1,0:T(8,128)(2,1)} custom-call(bf16[1024,128]{1,0:T(8,128)(2,1)} %get-tuple-element.73.refs_0_, bf16[1024,128]{1,0:T(8,128)(2,1)} %copy-done.7, bf16[1024,128]{1,0:T(8,128)(2,1)} %copy-done.11, bf16[1024,128]{1,0:T(8,128)(2,1)} %copy-done.10, bf16[1024,128]{1,0:T(8,128)(2,1)} %copy-done.12, ...), custom_call_target="tpu_custom_call" | custom-call | flops 6039797760 | bytes 25165824 | tf_op jit(solution)/shard_map/pallas_call | solution.py:262
  115.9 0.7 copy-done.2
  116.7 0.7 copy-done.5
  117.4 10.2 %shard_map.69.refs_5_ = bf16[128,128,128]{2,1,0:T(8,128)(2,1)} custom-call(bf16[1024,128]{1,0:T(8,128)(2,1)} %copy-done.1, bf16[1024,128]{1,0:T(8,128)(2,1)} %copy-done.5, bf16[1024,128]{1,0:T(8,128)(2,1)} %copy-done.3, bf16[1024,128]{1,0:T(8,128)(2,1)} %copy-done.2, bf16[128,768]{1,0:T(8,128)(2,1)} %get-tuple-element.54.refs_10_.refs_4_.refs_2_, ...), custom_call_target="tpu_custom_call" | custom-call | flops 2415919104 | bytes 25165824 | tf_op jit(solution)/shard_map/pallas_call | solution.py:262
  127.6 0.7 copy-done.4
  128.3 0.7 copy-done.6
  129.0 8.3 %shard_map.70 = bf16[128,128,128]{2,1,0:T(8,128)(2,1)} custom-call(bf16[1024,128]{1,0:T(8,128)(2,1)} %copy-done.6, bf16[1024,128]{1,0:T(8,128)(2,1)} %copy-done.4, bf16[128,768]{1,0:T(8,128)(2,1)} %get-tuple-element.54.refs_10_.refs_4_.refs_2_, bf16[768,128]{1,0:T(8,128)(2,1)} %get-tuple-element.55.refs_11_.refs_5_.refs_3_, ...), custom_call_target="tpu_custom_call" | custom-call | flops 1207959552 | bytes 25165824 | tf_op jit(solution)/shard_map/pallas_call | solution.py:262
  (40 shorter events, 1.2 us)
Async XLA Ops:
  4.0 90.3 %all-to-all-start = ((bf16[16,144,128]{2,1,0:T(8,128)(2,1)}), bf16[16,144,128]{2,1,0:T(8,128)(2,1)S(1)}, u32[]{:S(2)}, u32[]{:S(2)}) async-start(bf16[16,144,128]{2,1,0:T(8,128)(2,1)} %shard_map.66), calls=%async_computation | async-start | bytes 1179648 | tf_op jit(solution)/shard_map/all_to_all | solution.py:290
  13.8 8.9 %collective-permute-start.12 = (bf16[1024,128]{1,0:T(8,128)(2,1)}, bf16[1024,128]{1,0:T(8,128)(2,1)S(1)}, u32[]{:S(2)}, u32[]{:S(2)}) collective-permute-start(bf16[1024,128]{1,0:T(8,128)(2,1)} %get-tuple-element.70), channel_id=1, source_target_pairs={{0,1},{1,0},{2,3},{3,2},{4,5},{5,4},{6,7},{7,6},{8,9},{9,8},{10,11... | collective-permute-start | bytes 786440 | tf_op jit(solution)/shard_map/ppermute | solution.py:299
  14.2 29.7 %collective-permute-start.9 = (bf16[1024,128]{1,0:T(8,128)(2,1)}, bf16[1024,128]{1,0:T(8,128)(2,1)S(1)}, u32[]{:S(2)}, u32[]{:S(2)}) collective-permute-start(bf16[1024,128]{1,0:T(8,128)(2,1)} %get-tuple-element.65), channel_id=1, source_target_pairs={{0,9},{1,8},{2,11},{3,10},{4,13},{5,12},{6,15},{7,14},{8,1},{9,0},... | collective-permute-start | bytes 786440 | tf_op jit(solution)/shard_map/ppermute | solution.py:299
  16.3 38.2 %collective-permute-start.6 = (bf16[1024,128]{1,0:T(8,128)(2,1)}, bf16[1024,128]{1,0:T(8,128)(2,1)S(1)}, u32[]{:S(2)}, u32[]{:S(2)}) collective-permute-start(bf16[1024,128]{1,0:T(8,128)(2,1)} %get-tuple-element.60), channel_id=1, source_target_pairs={{0,8},{1,9},{2,10},{3,11},{4,12},{5,13},{6,14},{7,15},{8,0},{9,1},... | collective-permute-start | bytes 786440 | tf_op jit(solution)/shard_map/ppermute | solution.py:299
  16.6 37.9 %collective-permute-start.3 = (bf16[1024,128]{1,0:T(8,128)(2,1)}, bf16[1024,128]{1,0:T(8,128)(2,1)S(1)}, u32[]{:S(2)}, u32[]{:S(2)}) collective-permute-start(bf16[1024,128]{1,0:T(8,128)(2,1)} %get-tuple-element.51), channel_id=1, source_target_pairs={{0,3},{1,2},{2,1},{3,0},{4,7},{5,6},{6,5},{7,4},{8,11},{9,10},{10,... | collective-permute-start | bytes 786440 | tf_op jit(solution)/shard_map/ppermute | solution.py:299
  16.9 39.9 %collective-permute-start = (bf16[1024,128]{1,0:T(8,128)(2,1)}, bf16[1024,128]{1,0:T(8,128)(2,1)S(1)}, u32[]{:S(2)}, u32[]{:S(2)}) collective-permute-start(bf16[1024,128]{1,0:T(8,128)(2,1)} %get-tuple-element.46), channel_id=1, source_target_pairs={{0,2},{1,3},{2,0},{3,1},{4,6},{5,7},{6,4},{7,5},{8,10},{9,11},{10,... | collective-permute-start | bytes 786440 | tf_op jit(solution)/shard_map/ppermute | solution.py:299
  22.7 75.4 %copy-start.7 = (bf16[1024,128]{1,0:T(8,128)(2,1)}, bf16[1024,128]{1,0:T(8,128)(2,1)S(1)}, u32[]{:S(2)}) copy-start(bf16[1024,128]{1,0:T(8,128)(2,1)S(1)} %collective-permute-done.12.refs_1_) | copy-start | bytes 786436
  22.7 35.3 %collective-permute-start.13 = (bf16[1024,128]{1,0:T(8,128)(2,1)}, bf16[1024,128]{1,0:T(8,128)(2,1)S(1)}, u32[]{:S(2)}, u32[]{:S(2)}) collective-permute-start(bf16[1024,128]{1,0:T(8,128)(2,1)} %get-tuple-element.71), channel_id=1, source_target_pairs={{0,4},{1,5},{2,6},{3,7},{4,0},{5,1},{6,2},{7,3},{8,12},{9,13},{10,... | collective-permute-start | bytes 786440 | tf_op jit(solution)/shard_map/ppermute | solution.py:299
  43.9 54.2 %copy-start.8 = (bf16[1024,128]{1,0:T(8,128)(2,1)}, bf16[1024,128]{1,0:T(8,128)(2,1)S(1)}, u32[]{:S(2)}) copy-start(bf16[1024,128]{1,0:T(8,128)(2,1)S(1)} %collective-permute-done.9.refs_7_) | copy-start | bytes 786436
  43.9 22.6 %collective-permute-start.10 = (bf16[1024,128]{1,0:T(8,128)(2,1)}, bf16[1024,128]{1,0:T(8,128)(2,1)S(1)}, u32[]{:S(2)}, u32[]{:S(2)}) collective-permute-start(bf16[1024,128]{1,0:T(8,128)(2,1)} %get-tuple-element.66), channel_id=1, source_target_pairs={{0,11},{1,10},{2,9},{3,8},{4,15},{5,14},{6,13},{7,12},{8,3},{9,2},... | collective-permute-start | bytes 786440 | tf_op jit(solution)/shard_map/ppermute | solution.py:299
  54.5 43.7 %copy-start.9 = (bf16[1024,128]{1,0:T(8,128)(2,1)}, bf16[1024,128]{1,0:T(8,128)(2,1)S(1)}, u32[]{:S(2)}) copy-start(bf16[1024,128]{1,0:T(8,128)(2,1)S(1)} %collective-permute-done.6.refs_6_) | copy-start | bytes 786436
  54.5 16.9 %collective-permute-start.7 = (bf16[1024,128]{1,0:T(8,128)(2,1)}, bf16[1024,128]{1,0:T(8,128)(2,1)S(1)}, u32[]{:S(2)}, u32[]{:S(2)}) collective-permute-start(bf16[1024,128]{1,0:T(8,128)(2,1)} %get-tuple-element.61), channel_id=1, source_target_pairs={{0,10},{1,11},{2,8},{3,9},{4,14},{5,15},{6,12},{7,13},{8,2},{9,3},... | collective-permute-start | bytes 786440 | tf_op jit(solution)/shard_map/ppermute | solution.py:299
  54.5 43.7 %copy-start.10 = (bf16[1024,128]{1,0:T(8,128)(2,1)}, bf16[1024,128]{1,0:T(8,128)(2,1)S(1)}, u32[]{:S(2)}) copy-start(bf16[1024,128]{1,0:T(8,128)(2,1)S(1)} %collective-permute-done.3.refs_3_) | copy-start | bytes 786436
  54.5 16.9 %collective-permute-start.4 = (bf16[1024,128]{1,0:T(8,128)(2,1)}, bf16[1024,128]{1,0:T(8,128)(2,1)S(1)}, u32[]{:S(2)}, u32[]{:S(2)}) collective-permute-start(bf16[1024,128]{1,0:T(8,128)(2,1)} %get-tuple-element.52), channel_id=1, source_target_pairs={{0,6},{1,7},{2,4},{3,5},{4,2},{5,3},{6,0},{7,1},{8,14},{9,15},{10,... | collective-permute-start | bytes 786440 | tf_op jit(solution)/shard_map/ppermute | solution.py:299
  56.8 41.3 %copy-start.11 = (bf16[1024,128]{1,0:T(8,128)(2,1)}, bf16[1024,128]{1,0:T(8,128)(2,1)S(1)}, u32[]{:S(2)}) copy-start(bf16[1024,128]{1,0:T(8,128)(2,1)S(1)} %collective-permute-done.refs_2_) | copy-start | bytes 786436
  56.8 34.5 %collective-permute-start.1 = (bf16[1024,128]{1,0:T(8,128)(2,1)}, bf16[1024,128]{1,0:T(8,128)(2,1)S(1)}, u32[]{:S(2)}, u32[]{:S(2)}) collective-permute-start(bf16[1024,128]{1,0:T(8,128)(2,1)} %get-tuple-element.47), channel_id=1, source_target_pairs={{0,5},{1,4},{2,7},{3,6},{4,1},{5,0},{6,3},{7,2},{8,13},{9,12},{10,... | collective-permute-start | bytes 786440 | tf_op jit(solution)/shard_map/ppermute | solution.py:299
  58.0 0.7 copy-start.12
  58.7 57.2 %collective-permute-start.14 = (bf16[1024,128]{1,0:T(8,128)(2,1)}, bf16[1024,128]{1,0:T(8,128)(2,1)S(1)}, u32[]{:S(2)}, u32[]{:S(2)}) collective-permute-start(bf16[1024,128]{1,0:T(8,128)(2,1)} %get-tuple-element.72), channel_id=1, source_target_pairs={{0,13},{1,12},{2,15},{3,14},{4,9},{5,8},{6,11},{7,10},{8,5},{9,4},... | collective-permute-start | bytes 786440 | tf_op jit(solution)/shard_map/ppermute | solution.py:299
  66.5 0.7 copy-start.13
  67.2 48.7 %collective-permute-start.11 = (bf16[1024,128]{1,0:T(8,128)(2,1)}, bf16[1024,128]{1,0:T(8,128)(2,1)S(1)}, u32[]{:S(2)}, u32[]{:S(2)}) collective-permute-start(bf16[1024,128]{1,0:T(8,128)(2,1)} %get-tuple-element.67), channel_id=1, source_target_pairs={{0,12},{1,13},{2,14},{3,15},{4,8},{5,9},{6,10},{7,11},{8,4},{9,5},... | collective-permute-start | bytes 786440 | tf_op jit(solution)/shard_map/ppermute | solution.py:299
  71.4 0.7 copy-start.14
  71.4 44.5 %collective-permute-start.8 = (bf16[1024,128]{1,0:T(8,128)(2,1)}, bf16[1024,128]{1,0:T(8,128)(2,1)S(1)}, u32[]{:S(2)}, u32[]{:S(2)}) collective-permute-start(bf16[1024,128]{1,0:T(8,128)(2,1)} %get-tuple-element.62), channel_id=1, source_target_pairs={{0,7},{1,6},{2,5},{3,4},{4,3},{5,2},{6,1},{7,0},{8,15},{9,14},{10,... | collective-permute-start | bytes 786440 | tf_op jit(solution)/shard_map/ppermute | solution.py:299
  72.1 43.8 %copy-start.1 = (bf16[1024,128]{1,0:T(8,128)(2,1)}, bf16[1024,128]{1,0:T(8,128)(2,1)S(1)}, u32[]{:S(2)}) copy-start(bf16[1024,128]{1,0:T(8,128)(2,1)S(1)} %collective-permute-done.4.refs_0_) | copy-start | bytes 786436
  72.1 55.5 %collective-permute-start.5 = (bf16[1024,128]{1,0:T(8,128)(2,1)}, bf16[1024,128]{1,0:T(8,128)(2,1)S(1)}, u32[]{:S(2)}, u32[]{:S(2)}) collective-permute-start(bf16[1024,128]{1,0:T(8,128)(2,1)} %get-tuple-element.53), channel_id=1, source_target_pairs={{0,15},{1,14},{2,13},{3,12},{4,11},{5,10},{6,9},{7,8},{8,7},{9,6},... | collective-permute-start | bytes 786440 | tf_op jit(solution)/shard_map/ppermute | solution.py:299
  91.4 0.7 copy-start.15
  92.1 35.5 %collective-permute-start.2 = (bf16[1024,128]{1,0:T(8,128)(2,1)}, bf16[1024,128]{1,0:T(8,128)(2,1)S(1)}, u32[]{:S(2)}, u32[]{:S(2)}) collective-permute-start(bf16[1024,128]{1,0:T(8,128)(2,1)} %get-tuple-element.48), channel_id=1, source_target_pairs={{0,14},{1,15},{2,12},{3,13},{4,10},{5,11},{6,8},{7,9},{8,6},{9,7},... | collective-permute-start | bytes 786440 | tf_op jit(solution)/shard_map/ppermute | solution.py:299
  94.3 0.8 copy-start
  115.9 0.7 copy-start.2
  115.9 0.8 copy-start.3
  116.7 0.7 copy-start.5
  127.6 0.7 copy-start.4
  128.3 0.7 copy-start.6

commit v2 on v1

--- a/solution.py
+++ b/solution.py
@@ -12,10 +12,10 @@
 UNIT_ROWS = 16
 B_BLOCK = 64
 ACC = jnp.bfloat16
-SENT = (4, 0, 1, 5, 2, 3, 6, 7)
-GROUPS = ((0, 1, 2, 4, 5), (3, 6), (7,))
-IN_FLIGHT = 5
-VMEM = 56 * 1024 * 1024
+GROUPS = ((0, 1, 2, 3, 4), (5, 6), (7,))
+FAR_AHEAD = 3
+NEAR_AHEAD = 2
+VMEM = 60 * 1024 * 1024
 
 
 def pieces_kernel(shifts, ids_ref, source_ref, *refs):
@@ -45,7 +45,7 @@
 
 def matrices_kernel(workers, counts_ref, matrix_ids_ref, peramb_ref, matrix_ref, choice_ref, spread_ref):
     rows = MOST * LEGS
-    diagrams = matrix_ids_ref.shape[0]
+    diagrams = matrix_ids_ref.shape[1]
     total = peramb_ref.shape[0]
     lanes = lax.broadcasted_iota(jnp.int32, (1, total), 1)
 
@@ -54,7 +54,7 @@
             diagram = jnp.minimum(start + slot, diagrams - 1)
             for leg in range(LEGS):
                 choice_ref[pl.ds(sink * rows + slot * LEGS + leg, 1), :] = jnp.where(
-                    lanes == matrix_ids_ref[diagram, leg], 1.0, 0.0
+                    lanes == matrix_ids_ref[leg, diagram], 1.0, 0.0
                 )
         return start + counts_ref[sink]
 
@@ -86,7 +86,7 @@
             pltpu.VMEM((workers * rows * a_per, extent), jnp.float32),
         ],
         compiler_params=pltpu.CompilerParams(vmem_limit_bytes=VMEM),
-    )(sink_counts, peramb_ids, perambs)
+    )(sink_counts, peramb_ids.T, perambs)
 
 
 def legs_kernel(
@@ -281,26 +281,42 @@
     workers = lax.axis_size("work")
     extent = sources.shape[2]
     per_unit = UNIT_ROWS * workers // extent
-    order = [u * per_unit + lane for u in SENT for lane in range(per_unit)]
-    order.remove(0)
-    early, late = tuple(order[:IN_FLIGHT]), (0, *order[IN_FLIGHT:])
+    half = workers // 2
+    far = list(range(half, workers))
+    near = [1, *range(half // 2, half), *range(2, half // 2)]
+    early = (*far[:FAR_AHEAD], *near[:NEAR_AHEAD])
+    late = (0, *far[FAR_AHEAD:], *near[NEAR_AHEAD:])
     pieces = dict(zip(early, choose_pieces(sources, source_ids, early)))
     pieces.update(zip(late, choose_pieces(sources, source_ids, late)))
+    arrived = {0: pieces[0]}
+
+    def send(shift, *after):
+        piece = pieces[shift]
+        for before in after:
+            piece, arrived[before] = lax.optimization_barrier((piece, arrived[before]))
+        arrived[shift] = lax.ppermute(piece, "work", [(i, i ^ shift) for i in range(workers)])
+
+    for shift in early:
+        send(shift)
     matrices = choose_matrices(perambs, peramb_ids, sink_counts, workers, extent)
+    matrices, arrived[1] = lax.optimization_barrier((matrices, arrived[1]))
     matrices = lax.all_to_all(matrices, "work", split_axis=0, concat_axis=0, tiled=True)
     leg3, leg2, leg1 = make_legs(matrices, sink_counts, weights, workers)
-
-    arrived = {0: pieces[0]}
-    for place, shift in enumerate(order):
-        piece = pieces[shift]
-        if place >= IN_FLIGHT:
-            before = order[place - IN_FLIGHT]
-            piece, arrived[before] = lax.optimization_barrier((piece, arrived[before]))
-        arrived[shift] = lax.ppermute(piece, "work", [(i, i ^ shift) for i in range(workers)])
+    for place in range(NEAR_AHEAD, len(near)):
+        send(near[place], near[place - NEAR_AHEAD])
+
     acc = None
+    sent = FAR_AHEAD
     for group, units in enumerate(GROUPS):
-        members = [arrived[u * per_unit + lane] for u in units for lane in range(per_unit)]
-        acc = add_group(units, members, leg3, leg2, leg1, acc, group == len(GROUPS) - 1)
+        last = group == len(GROUPS) - 1
+        members = [u * per_unit + lane for u in units for lane in range(per_unit)]
+        wanted = len(far) if last else far.index(max(members)) + 1 + FAR_AHEAD
+        while sent < min(wanted, len(far)):
+            send(far[sent], far[sent - FAR_AHEAD])
+            sent += 1
+        acc = add_group(units, [arrived[m] for m in members], leg3, leg2, leg1, acc, last)
+        if sent < len(far):
+            pieces[far[sent]], acc = lax.optimization_barrier((pieces[far[sent]], acc))
     return acc.reshape(1, extent * extent, extent)
 
 

time: 138 us -> 141 us (1.022)
  the two profiles are of different devices: /device:TPU:5 before, /device:TPU:11 now
where the time goes in v2:
time: 141 us; the launch traced here: 139 us
  waiting for transfers between devices  56.6 us (40%)
  Pallas kernels  48.9 us (35%)
  starting transfers between devices  31 us (22%)
  local copies, waits for them, and re-layouts  2.75 us (2%)
    ppermute x15, waiting for transfers between devices, send(): lax.ppermute(piece, 'work', [(i, i ^ shift) for i in range(workers)])  56.6 us
    pallas_call x3, Pallas kernels, add_group(): pl.pallas_call(functools.partial(group_kernel, first, last, units, per_un...  36.1 us
    ppermute x15, starting transfers between devices, send(): lax.ppermute(piece, 'work', [(i, i ^ shift) for i in range(workers)])  25 us
    pallas_call x2, Pallas kernels, choose_pieces(): pl.pallas_call(functools.partial(pieces_kernel, shifts), in_specs=[pl.Blo...  7.17 us
    all_to_all x1, starting transfers between devices, per_device(): lax.all_to_all(matrices, 'work', split_axis=0, concat_axis=0, tiled=True)  6.05 us
    pallas_call x1, Pallas kernels, make_legs(): pl.pallas_call(functools.partial(legs_kernel, workers), in_specs=[smem, s...  3 us
  transfers between devices with their start and end apart: 16, of which 7 were waited for; matrix products, arithmetic and copies ran while one was open for 0% of the time, Pallas kernels for 27%

profile of v2, /device:TPU:11, one launch (start us, length us, event | category | flops | bytes accessed | tf_op | source)
XLA Modules:
  0.0 139.5 jit_solution(10540482259687734912)
XLA Ops:
  0.0 3.0 %shard_map.65 = (bf16[1024,128]{1,0:T(8,128)(2,1)}, bf16[1024,128]{1,0:T(8,128)(2,1)}, bf16[1024,128]{1,0:T(8,128)(2,1)}, bf16[1024,128]{1,0:T(8,128)(2,1)}, bf16[1024,128]{1,0:T(8,128)(2,1)}) custom-call(s32[16]{0:T(128)} %ids_ref.3, bf16[16,1024,128]{2,1,0:T(8,128)(2,1)} %source_ref.3), custom_call_target="tpu_custom_call" | custom-call | tf_op jit(solution)/shard_map/pallas_call | solution.py:36
  3.1 0.7 collective-permute-start.6
  3.8 2.6 %shard_map.66 = bf16[16,144,128]{2,1,0:T(8,128)(2,1)} custom-call(s32[16]{0:T(128)} %counts_ref.3, s32[3,48]{1,0:T(4,128)} %bitcast.2, bf16[96,1024]{1,0:T(8,128)(2,1)} %peramb_ref.1), custom_call_target="tpu_custom_call" | custom-call | tf_op jit(solution)/shard_map/pallas_call | solution.py:79
  6.4 6.1 %all-to-all-start = ((bf16[16,144,128]{2,1,0:T(8,128)(2,1)}), bf16[16,144,128]{2,1,0:T(8,128)(2,1)S(1)}, u32[]{:S(2)}, u32[]{:S(2)}) async-start(bf16[16,144,128]{2,1,0:T(8,128)(2,1)} %shard_map.66), calls=%async_computation | async-start | bytes 1179648 | tf_op jit(solution)/shard_map/all_to_all | solution.py:303
  12.5 0.1 collective-permute-start.7
  12.5 4.1 %shard_map.64 = (bf16[1024,128]{1,0:T(8,128)(2,1)}, bf16[1024,128]{1,0:T(8,128)(2,1)}, bf16[1024,128]{1,0:T(8,128)(2,1)}, bf16[1024,128]{1,0:T(8,128)(2,1)}, bf1...) custom-call(s32[16]{0:T(128)} %ids_ref.3, ...), custom_call_target="tpu_custom_call" | custom-call | tf_op jit(solution)/shard_map/pallas_call | solution.py:36
  16.7 2.0 %collective-permute-start.10 = (bf16[1024,128]{1,0:T(8,128)(2,1)}, bf16[1024,128]{1,0:T(8,128)(2,1)S(1)}, u32[]{:S(2)}, u32[]{:S(2)}) collective-permute-start(bf16[1024,128]{1,0:T(8,128)(2,1)} %get-tuple-element.75), channel_id=1, source_target_pairs={{0,5},{1,4},{2,7},{3,6},{4,1},{5,0},{6,3},{7,2},{8,13},{9,12},{10,... | collective-permute-start | bytes 786440 | tf_op jit(solution)/shard_map/ppermute | solution.py:297
  18.6 10.3 %collective-permute-done.7.refs_4_ = bf16[1024,128]{1,0:T(8,128)(2,1)S(1)} collective-permute-done((bf16[1024,128]{1,0:T(8,128)(2,1)}, bf16[1024,128]{1,0:T(8,128)(2,1)S(1)}, u32[]{:S(2)}, u32[]{:S(2)}) %collective-permute-start.7) | collective-permute-done | bytes 262176 | tf_op jit(solution)/shard_map/ppermute | solution.py:297
  29.0 1.9 %collective-permute-start.8 = (bf16[1024,128]{1,0:T(8,128)(2,1)}, bf16[1024,128]{1,0:T(8,128)(2,1)S(1)}, u32[]{:S(2)}, u32[]{:S(2)}) collective-permute-start(bf16[1024,128]{1,0:T(8,128)(2,1)} %get-tuple-element.71), channel_id=1, source_target_pairs={{0,6},{1,7},{2,4},{3,5},{4,2},{5,3},{6,0},{7,1},{8,14},{9,15},{10,... | collective-permute-start | bytes 786440 | tf_op jit(solution)/shard_map/ppermute | solution.py:297
  30.9 3.8 %collective-permute-done.10.refs_5_ = bf16[1024,128]{1,0:T(8,128)(2,1)S(1)} collective-permute-done((bf16[1024,128]{1,0:T(8,128)(2,1)}, bf16[1024,128]{1,0:T(8,128)(2,1)S(1)}, u32[]{:S(2)}, u32[]{:S(2)}) %collective-permute-start.10) | collective-permute-done | bytes 262176 | tf_op jit(solution)/shard_map/ppermute | solution.py:297
  34.7 2.1 %collective-permute-start.11 = (bf16[1024,128]{1,0:T(8,128)(2,1)}, bf16[1024,128]{1,0:T(8,128)(2,1)S(1)}, u32[]{:S(2)}, u32[]{:S(2)}) collective-permute-start(bf16[1024,128]{1,0:T(8,128)(2,1)} %get-tuple-element.76), channel_id=1, source_target_pairs={{0,7},{1,6},{2,5},{3,4},{4,3},{5,2},{6,1},{7,0},{8,15},{9,14},{10,... | collective-permute-start | bytes 786440 | tf_op jit(solution)/shard_map/ppermute | solution.py:297
  36.8 2.2 %collective-permute-start = (bf16[1024,128]{1,0:T(8,128)(2,1)S(1)}, bf16[1024,128]{1,0:T(8,128)(2,1)S(1)}, u32[]{:S(2)}, u32[]{:S(2)}) collective-permute-start(bf16[1024,128]{1,0:T(8,128)(2,1)S(1)} %copy-done.15), channel_id=1, source_target_pairs={{0,8},{1,9},{2,10},{3,11},{4,12},{5,13},{6,14},{7,15},{8,0},{9,1},... | collective-permute-start | bytes 786440 | tf_op jit(solution)/shard_map/ppermute | solution.py:297
  39.0 1.1 collective-permute-start.3
  40.1 7.1 %collective-permute-done.8.refs_6_ = bf16[1024,128]{1,0:T(8,128)(2,1)S(1)} collective-permute-done((bf16[1024,128]{1,0:T(8,128)(2,1)}, bf16[1024,128]{1,0:T(8,128)(2,1)S(1)}, u32[]{:S(2)}, u32[]{:S(2)}) %collective-permute-start.8) | collective-permute-done | bytes 262176 | tf_op jit(solution)/shard_map/ppermute | solution.py:297
  47.2 2.4 %collective-permute-start.9 = (bf16[1024,128]{1,0:T(8,128)(2,1)}, bf16[1024,128]{1,0:T(8,128)(2,1)}, u32[]{:S(2)}, u32[]{:S(2)}) collective-permute-start(bf16[1024,128]{1,0:T(8,128)(2,1)} %get-tuple-element.72), channel_id=1, source_target_pairs={{0,2},{1,3},{2,0},{3,1},{4,6},{5,7},{6,4},{7,5},{8,10},{9,11},{10,... | collective-permute-start | bytes 786440 | tf_op jit(solution)/shard_map/ppermute | solution.py:297
  49.6 3.8 %collective-permute-done.11.refs_7_ = bf16[1024,128]{1,0:T(8,128)(2,1)S(1)} collective-permute-done((bf16[1024,128]{1,0:T(8,128)(2,1)}, bf16[1024,128]{1,0:T(8,128)(2,1)S(1)}, u32[]{:S(2)}, u32[]{:S(2)}) %collective-permute-start.11) | collective-permute-done | bytes 262176 | tf_op jit(solution)/shard_map/ppermute | solution.py:297
  53.4 2.7 %collective-permute-start.12 = (bf16[1024,128]{1,0:T(8,128)(2,1)}, bf16[1024,128]{1,0:T(8,128)(2,1)}, u32[]{:S(2)}, u32[]{:S(2)}) collective-permute-start(bf16[1024,128]{1,0:T(8,128)(2,1)} %get-tuple-element.77), channel_id=1, source_target_pairs={{0,3},{1,2},{2,1},{3,0},{4,7},{5,6},{6,5},{7,4},{8,11},{9,10},{10,... | collective-permute-start | bytes 786440 | tf_op jit(solution)/shard_map/ppermute | solution.py:297
  56.1 0.7 collective-permute-start.13
  56.8 9.6 %collective-permute-done.3.refs_9_ = bf16[1024,128]{1,0:T(8,128)(2,1)S(1)} collective-permute-done((bf16[1024,128]{1,0:T(8,128)(2,1)S(1)}, bf16[1024,128]{1,0:T(8,128)(2,1)S(1)}, u32[]{:S(2)}, u32[]{:S(2)}) %collective-permute-start.3) | collective-permute-done | bytes 262176 | tf_op jit(solution)/shard_map/ppermute | solution.py:297
  66.5 4.6 %collective-permute-start.1 = (bf16[1024,128]{1,0:T(8,128)(2,1)}, bf16[1024,128]{1,0:T(8,128)(2,1)S(1)}, u32[]{:S(2)}, u32[]{:S(2)}) collective-permute-start(bf16[1024,128]{1,0:T(8,128)(2,1)} %get-tuple-element.51), channel_id=1, source_target_pairs={{0,11},{1,10},{2,9},{3,8},{4,15},{5,14},{6,13},{7,12},{8,3},{9,2},... | collective-permute-start | bytes 786440 | tf_op jit(solution)/shard_map/ppermute | solution.py:297
  71.0 0.8 copy-done
  71.8 3.0 %shard_map.67 = (bf16[128,768]{1,0:T(8,128)(2,1)}, bf16[768,128]{1,0:T(8,128)(2,1)}, bf16[8,96,128]{2,1,0:T(8,128)(2,1)}) custom-call(s32[16]{0:T(128)} %counts_ref.3, f32[48]{0:T(128)} %weights_ref.1, bf16[16,144,128]{2,1,0:T(8,128)(2,1)} %copy-done), custom_call_target="tpu_custom_call" | custom-call | tf_op jit(solution)/shard_map/pallas_call | solution.py:135
  74.9 17.7 %shard_map.68.refs_7_ = bf16[128,128,128]{2,1,0:T(8,128)(2,1)} custom-call(bf16[1024,128]{1,0:T(8,128)(2,1)} %get-tuple-element.64.refs_0_, bf16[1024,128]{1,0:T(8,128)(2,1)} %copy-done.11, bf16[1024,128]{1,0:T(8,128)(2,1)} %collective-permute-done.9.refs_2_, bf16[1024,128]{1,0:T(8,128)(2,1)} %collective-permute-done.12.refs_3_, ...), custom_call_target="tpu_custom_call" | custom-call | flops 6039797760 | bytes 25165824 | tf_op jit(solution)/shard_map/pallas_call | solution.py:262
  92.7 3.4 %collective-permute-start.14 = (bf16[1024,128]{1,0:T(8,128)(2,1)S(1)}, bf16[1024,128]{1,0:T(8,128)(2,1)S(1)}, u32[]{:S(2)}, u32[]{:S(2)}) collective-permute-start(bf16[1024,128]{1,0:T(8,128)(2,1)S(1)} %copy-done.10), channel_id=1, source_target_pairs={{0,13},{1,12},{2,15},{3,14},{4,9},{5,8},{6,11},{7,10},{8,5},{9,4},... | collective-permute-start | bytes 786440 | tf_op jit(solution)/shard_map/ppermute | solution.py:297
  96.1 1.0 collective-permute-start.5
  97.2 21.8 %collective-permute-done.14.refs_3_ = bf16[1024,128]{1,0:T(8,128)(2,1)S(1)} collective-permute-done((bf16[1024,128]{1,0:T(8,128)(2,1)S(1)}, bf16[1024,128]{1,0:T(8,128)(2,1)S(1)}, u32[]{:S(2)}, u32[]{:S(2)}) %collective-permute-start.14) | collective-permute-done | bytes 262176 | tf_op jit(solution)/shard_map/ppermute | solution.py:297
  119.0 0.7 copy-done.5
  119.6 10.1 %shard_map.69.refs_5_ = bf16[128,128,128]{2,1,0:T(8,128)(2,1)} custom-call(bf16[1024,128]{1,0:T(8,128)(2,1)} %copy-done.1, bf16[1024,128]{1,0:T(8,128)(2,1)} %copy-done.3, bf16[1024,128]{1,0:T(8,128)(2,1)} %copy-done.2, bf16[1024,128]{1,0:T(8,128)(2,1)} %copy-done.5, bf16[128,768]{1,0:T(8,128)(2,1)} %get-tuple-element.60.refs_10_.refs_4_.refs_2_, ...), custom_call_target="tpu_custom_call" | custom-call | flops 2415919104 | bytes 25165824 | tf_op jit(solution)/shard_map/pallas_call | solution.py:262
  129.8 0.2 collective-permute-done.2.refs_0_
  130.0 0.5 copy-done.4
  130.5 0.7 copy-done.6
  131.2 8.3 %shard_map.70 = bf16[128,128,128]{2,1,0:T(8,128)(2,1)} custom-call(bf16[1024,128]{1,0:T(8,128)(2,1)} %copy-done.6, bf16[1024,128]{1,0:T(8,128)(2,1)} %copy-done.4, bf16[128,768]{1,0:T(8,128)(2,1)} %get-tuple-element.60.refs_10_.refs_4_.refs_2_, bf16[768,128]{1,0:T(8,128)(2,1)} %get-tuple-element.61.refs_11_.refs_5_.refs_3_, ...), custom_call_target="tpu_custom_call" | custom-call | flops 1207959552 | bytes 25165824 | tf_op jit(solution)/shard_map/pallas_call | solution.py:262
  (47 shorter events, 0.2 us)
Async XLA Ops:
  3.1 33.7 %copy-start.15 = (bf16[1024,128]{1,0:T(8,128)(2,1)S(1)}, bf16[1024,128]{1,0:T(8,128)(2,1)}, u32[]{:S(2)}) copy-start(bf16[1024,128]{1,0:T(8,128)(2,1)} %get-tuple-element.50) | copy-start | bytes 786436
  3.1 36.0 %copy-start.13 = (bf16[1024,128]{1,0:T(8,128)(2,1)S(1)}, bf16[1024,128]{1,0:T(8,128)(2,1)}, u32[]{:S(2)}) copy-start(bf16[1024,128]{1,0:T(8,128)(2,1)} %get-tuple-element.55) | copy-start | bytes 786436
  3.1 53.1 %copy-start.9 = (bf16[1024,128]{1,0:T(8,128)(2,1)S(1)}, bf16[1024,128]{1,0:T(8,128)(2,1)}, u32[]{:S(2)}) copy-start(bf16[1024,128]{1,0:T(8,128)(2,1)} %get-tuple-element.85) | copy-start | bytes 786436
  3.1 3.3 %collective-permute-start.6 = (bf16[1024,128]{1,0:T(8,128)(2,1)}, bf16[1024,128]{1,0:T(8,128)(2,1)S(1)}, u32[]{:S(2)}, u32[]{:S(2)}) collective-permute-start(bf16[1024,128]{1,0:T(8,128)(2,1)} %get-tuple-element.58), channel_id=1, source_target_pairs={{0,1},{1,0},{2,3},{3,2},{4,5},{5,4},{6,7},{7,6},{8,9},{9,8},{10,11... | collective-permute-start | bytes 786440 | tf_op jit(solution)/shard_map/ppermute | solution.py:297
  6.4 68.5 %copy-start.11 = (bf16[1024,128]{1,0:T(8,128)(2,1)}, bf16[1024,128]{1,0:T(8,128)(2,1)S(1)}, u32[]{:S(2)}) copy-start(bf16[1024,128]{1,0:T(8,128)(2,1)S(1)} %collective-permute-done.6.refs_1_) | copy-start | bytes 786436
  6.4 64.6 %all-to-all-start = ((bf16[16,144,128]{2,1,0:T(8,128)(2,1)}), bf16[16,144,128]{2,1,0:T(8,128)(2,1)S(1)}, u32[]{:S(2)}, u32[]{:S(2)}) async-start(bf16[16,144,128]{2,1,0:T(8,128)(2,1)} %shard_map.66), calls=%async_computation | async-start | bytes 1179648 | tf_op jit(solution)/shard_map/all_to_all | solution.py:303
  12.5 16.5 %collective-permute-start.7 = (bf16[1024,128]{1,0:T(8,128)(2,1)}, bf16[1024,128]{1,0:T(8,128)(2,1)S(1)}, u32[]{:S(2)}, u32[]{:S(2)}) collective-permute-start(bf16[1024,128]{1,0:T(8,128)(2,1)} %get-tuple-element.70), channel_id=1, source_target_pairs={{0,4},{1,5},{2,6},{3,7},{4,0},{5,1},{6,2},{7,3},{8,12},{9,13},{10,... | collective-permute-start | bytes 786440 | tf_op jit(solution)/shard_map/ppermute | solution.py:297
  16.7 18.0 %collective-permute-start.10 = (bf16[1024,128]{1,0:T(8,128)(2,1)}, bf16[1024,128]{1,0:T(8,128)(2,1)S(1)}, u32[]{:S(2)}, u32[]{:S(2)}) collective-permute-start(bf16[1024,128]{1,0:T(8,128)(2,1)} %get-tuple-element.75), channel_id=1, source_target_pairs={{0,5},{1,4},{2,7},{3,6},{4,1},{5,0},{6,3},{7,2},{8,13},{9,12},{10,... | collective-permute-start | bytes 786440 | tf_op jit(solution)/shard_map/ppermute | solution.py:297
  29.0 45.9 %copy-start.12 = (bf16[1024,128]{1,0:T(8,128)(2,1)}, bf16[1024,128]{1,0:T(8,128)(2,1)S(1)}, u32[]{:S(2)}) copy-start(bf16[1024,128]{1,0:T(8,128)(2,1)S(1)} %collective-permute-done.7.refs_4_) | copy-start | bytes 786436
  29.0 18.2 %collective-permute-start.8 = (bf16[1024,128]{1,0:T(8,128)(2,1)}, bf16[1024,128]{1,0:T(8,128)(2,1)S(1)}, u32[]{:S(2)}, u32[]{:S(2)}) collective-permute-start(bf16[1024,128]{1,0:T(8,128)(2,1)} %get-tuple-element.71), channel_id=1, source_target_pairs={{0,6},{1,7},{2,4},{3,5},{4,2},{5,3},{6,0},{7,1},{8,14},{9,15},{10,... | collective-permute-start | bytes 786440 | tf_op jit(solution)/shard_map/ppermute | solution.py:297
  34.7 40.2 %copy-start.14 = (bf16[1024,128]{1,0:T(8,128)(2,1)}, bf16[1024,128]{1,0:T(8,128)(2,1)S(1)}, u32[]{:S(2)}) copy-start(bf16[1024,128]{1,0:T(8,128)(2,1)S(1)} %collective-permute-done.10.refs_5_) | copy-start | bytes 786436
  34.7 18.7 %collective-permute-start.11 = (bf16[1024,128]{1,0:T(8,128)(2,1)}, bf16[1024,128]{1,0:T(8,128)(2,1)S(1)}, u32[]{:S(2)}, u32[]{:S(2)}) collective-permute-start(bf16[1024,128]{1,0:T(8,128)(2,1)} %get-tuple-element.76), channel_id=1, source_target_pairs={{0,7},{1,6},{2,5},{3,4},{4,3},{5,2},{6,1},{7,0},{8,15},{9,14},{10,... | collective-permute-start | bytes 786440 | tf_op jit(solution)/shard_map/ppermute | solution.py:297
  36.8 20.0 %collective-permute-start = (bf16[1024,128]{1,0:T(8,128)(2,1)S(1)}, bf16[1024,128]{1,0:T(8,128)(2,1)S(1)}, u32[]{:S(2)}, u32[]{:S(2)}) collective-permute-start(bf16[1024,128]{1,0:T(8,128)(2,1)S(1)} %copy-done.15), channel_id=1, source_target_pairs={{0,8},{1,9},{2,10},{3,11},{4,12},{5,13},{6,14},{7,15},{8,0},{9,1},... | collective-permute-start | bytes 786440 | tf_op jit(solution)/shard_map/ppermute | solution.py:297
  39.0 27.4 %collective-permute-start.3 = (bf16[1024,128]{1,0:T(8,128)(2,1)S(1)}, bf16[1024,128]{1,0:T(8,128)(2,1)S(1)}, u32[]{:S(2)}, u32[]{:S(2)}) collective-permute-start(bf16[1024,128]{1,0:T(8,128)(2,1)S(1)} %copy-done.13), channel_id=1, source_target_pairs={{0,9},{1,8},{2,11},{3,10},{4,13},{5,12},{6,15},{7,14},{8,1},{9,0},... | collective-permute-start | bytes 786440 | tf_op jit(solution)/shard_map/ppermute | solution.py:297
  47.2 27.7 %copy-start.16 = (bf16[1024,128]{1,0:T(8,128)(2,1)}, bf16[1024,128]{1,0:T(8,128)(2,1)S(1)}, u32[]{:S(2)}) copy-start(bf16[1024,128]{1,0:T(8,128)(2,1)S(1)} %collective-permute-done.8.refs_6_) | copy-start | bytes 786436
  47.2 27.7 %collective-permute-start.9 = (bf16[1024,128]{1,0:T(8,128)(2,1)}, bf16[1024,128]{1,0:T(8,128)(2,1)}, u32[]{:S(2)}, u32[]{:S(2)}) collective-permute-start(bf16[1024,128]{1,0:T(8,128)(2,1)} %get-tuple-element.72), channel_id=1, source_target_pairs={{0,2},{1,3},{2,0},{3,1},{4,6},{5,7},{6,4},{7,5},{8,10},{9,11},{10,... | collective-permute-start | bytes 786440 | tf_op jit(solution)/shard_map/ppermute | solution.py:297
  53.4 21.5 %copy-start.17 = (bf16[1024,128]{1,0:T(8,128)(2,1)}, bf16[1024,128]{1,0:T(8,128)(2,1)S(1)}, u32[]{:S(2)}) copy-start(bf16[1024,128]{1,0:T(8,128)(2,1)S(1)} %collective-permute-done.11.refs_7_) | copy-start | bytes 786436
  53.4 21.4 %collective-permute-start.12 = (bf16[1024,128]{1,0:T(8,128)(2,1)}, bf16[1024,128]{1,0:T(8,128)(2,1)}, u32[]{:S(2)}, u32[]{:S(2)}) collective-permute-start(bf16[1024,128]{1,0:T(8,128)(2,1)} %get-tuple-element.77), channel_id=1, source_target_pairs={{0,3},{1,2},{2,1},{3,0},{4,7},{5,6},{6,5},{7,4},{8,11},{9,10},{10,... | collective-permute-start | bytes 786440 | tf_op jit(solution)/shard_map/ppermute | solution.py:297
  56.1 36.5 %collective-permute-start.13 = (bf16[1024,128]{1,0:T(8,128)(2,1)S(1)}, bf16[1024,128]{1,0:T(8,128)(2,1)S(1)}, u32[]{:S(2)}, u32[]{:S(2)}) collective-permute-start(bf16[1024,128]{1,0:T(8,128)(2,1)S(1)} %copy-done.9), channel_id=1, source_target_pairs={{0,10},{1,11},{2,8},{3,9},{4,14},{5,15},{6,12},{7,13},{8,2},{9,3},... | collective-permute-start | bytes 786440 | tf_op jit(solution)/shard_map/ppermute | solution.py:297
  56.8 9.6 %copy-start.18 = (bf16[1024,128]{1,0:T(8,128)(2,1)}, bf16[1024,128]{1,0:T(8,128)(2,1)S(1)}, u32[]{:S(2)}) copy-start(bf16[1024,128]{1,0:T(8,128)(2,1)S(1)} %collective-permute-done.refs_8_) | copy-start | bytes 786436
  66.5 8.4 %copy-start.19 = (bf16[1024,128]{1,0:T(8,128)(2,1)}, bf16[1024,128]{1,0:T(8,128)(2,1)S(1)}, u32[]{:S(2)}) copy-start(bf16[1024,128]{1,0:T(8,128)(2,1)S(1)} %collective-permute-done.3.refs_9_) | copy-start | bytes 786436
  66.5 29.6 %collective-permute-start.4 = (bf16[1024,128]{1,0:T(8,128)(2,1)}, bf16[1024,128]{1,0:T(8,128)(2,1)S(1)}, u32[]{:S(2)}, u32[]{:S(2)}) collective-permute-start(bf16[1024,128]{1,0:T(8,128)(2,1)} %get-tuple-element.56), channel_id=1, source_target_pairs={{0,12},{1,13},{2,14},{3,15},{4,8},{5,9},{6,10},{7,11},{8,4},{9,5},... | collective-permute-start | bytes 786440 | tf_op jit(solution)/shard_map/ppermute | solution.py:297
  66.5 30.6 %collective-permute-start.1 = (bf16[1024,128]{1,0:T(8,128)(2,1)}, bf16[1024,128]{1,0:T(8,128)(2,1)S(1)}, u32[]{:S(2)}, u32[]{:S(2)}) collective-permute-start(bf16[1024,128]{1,0:T(8,128)(2,1)} %get-tuple-element.51), channel_id=1, source_target_pairs={{0,11},{1,10},{2,9},{3,8},{4,15},{5,14},{6,13},{7,12},{8,3},{9,2},... | collective-permute-start | bytes 786440 | tf_op jit(solution)/shard_map/ppermute | solution.py:297
  74.9 17.8 %copy-start.10 = (bf16[1024,128]{1,0:T(8,128)(2,1)S(1)}, bf16[1024,128]{1,0:T(8,128)(2,1)}, u32[]{:S(2)}) copy-start(bf16[1024,128]{1,0:T(8,128)(2,1)} %get-tuple-element.89) | copy-start | bytes 786436
  74.9 21.2 %copy-start.8 = (bf16[1024,128]{1,0:T(8,128)(2,1)S(1)}, bf16[1024,128]{1,0:T(8,128)(2,1)}, u32[]{:S(2)}) copy-start(bf16[1024,128]{1,0:T(8,128)(2,1)} %get-tuple-element.57) | copy-start | bytes 786436
  74.9 22.2 %copy-start.7 = (bf16[1024,128]{1,0:T(8,128)(2,1)S(1)}, bf16[1024,128]{1,0:T(8,128)(2,1)}, u32[]{:S(2)}) copy-start(bf16[1024,128]{1,0:T(8,128)(2,1)} %get-tuple-element.52) | copy-start | bytes 786436
  92.7 26.3 %copy-start.1 = (bf16[1024,128]{1,0:T(8,128)(2,1)}, bf16[1024,128]{1,0:T(8,128)(2,1)S(1)}, u32[]{:S(2)}) copy-start(bf16[1024,128]{1,0:T(8,128)(2,1)S(1)} %collective-permute-done.13.refs_0_) | copy-start | bytes 786436
  92.7 26.2 %collective-permute-start.14 = (bf16[1024,128]{1,0:T(8,128)(2,1)S(1)}, bf16[1024,128]{1,0:T(8,128)(2,1)S(1)}, u32[]{:S(2)}, u32[]{:S(2)}) collective-permute-start(bf16[1024,128]{1,0:T(8,128)(2,1)S(1)} %copy-done.10), channel_id=1, source_target_pairs={{0,13},{1,12},{2,15},{3,14},{4,9},{5,8},{6,11},{7,10},{8,5},{9,4},... | collective-permute-start | bytes 786440 | tf_op jit(solution)/shard_map/ppermute | solution.py:297
  96.1 22.9 %copy-start.2 = (bf16[1024,128]{1,0:T(8,128)(2,1)}, bf16[1024,128]{1,0:T(8,128)(2,1)S(1)}, u32[]{:S(2)}) copy-start(bf16[1024,128]{1,0:T(8,128)(2,1)S(1)} %collective-permute-done.4.refs_2_) | copy-start | bytes 786436
  96.1 33.7 %collective-permute-start.5 = (bf16[1024,128]{1,0:T(8,128)(2,1)S(1)}, bf16[1024,128]{1,0:T(8,128)(2,1)S(1)}, u32[]{:S(2)}, u32[]{:S(2)}) collective-permute-start(bf16[1024,128]{1,0:T(8,128)(2,1)S(1)} %copy-done.8), channel_id=1, source_target_pairs={{0,15},{1,14},{2,13},{3,12},{4,11},{5,10},{6,9},{7,8},{8,7},{9,6},... | collective-permute-start | bytes 786440 | tf_op jit(solution)/shard_map/ppermute | solution.py:297
  97.1 21.8 %copy-start.3 = (bf16[1024,128]{1,0:T(8,128)(2,1)}, bf16[1024,128]{1,0:T(8,128)(2,1)S(1)}, u32[]{:S(2)}) copy-start(bf16[1024,128]{1,0:T(8,128)(2,1)S(1)} %collective-permute-done.1.refs_1_) | copy-start | bytes 786436
  97.1 32.9 %collective-permute-start.2 = (bf16[1024,128]{1,0:T(8,128)(2,1)S(1)}, bf16[1024,128]{1,0:T(8,128)(2,1)S(1)}, u32[]{:S(2)}, u32[]{:S(2)}) collective-permute-start(bf16[1024,128]{1,0:T(8,128)(2,1)S(1)} %copy-done.7), channel_id=1, source_target_pairs={{0,14},{1,15},{2,12},{3,13},{4,10},{5,11},{6,8},{7,9},{8,6},{9,7},... | collective-permute-start | bytes 786440 | tf_op jit(solution)/shard_map/ppermute | solution.py:297
  (4 other events, 2.9 us)

commit v3 on v2

--- a/solution.py
+++ b/solution.py
@@ -15,30 +15,39 @@
 GROUPS = ((0, 1, 2, 3, 4), (5, 6), (7,))
 FAR_AHEAD = 3
 NEAR_AHEAD = 2
-VMEM = 60 * 1024 * 1024
+VMEM = 46 * 1024 * 1024
 
 
 def pieces_kernel(shifts, ids_ref, source_ref, *refs):
-    piece_refs, sems = refs[: len(shifts)], refs[len(shifts)]
+    piece_refs, (held_ref, in_sems, out_sems) = refs[: len(shifts)], refs[len(shifts) :]
     own = lax.axis_index("work")
-    copies = []
+    reads, writes = [], []
     for i, shift in enumerate(shifts):
-        copy = pltpu.make_async_copy(
-            source_ref.at[ids_ref[own ^ shift]], piece_refs[i], sems.at[i]
+        reads.append(
+            pltpu.make_async_copy(
+                source_ref.at[ids_ref[own ^ shift]], held_ref.at[i], in_sems.at[i]
+            )
         )
-        copy.start()
-        copies.append(copy)
-    for copy in copies:
-        copy.wait()
+        writes.append(pltpu.make_async_copy(held_ref.at[i], piece_refs[i], out_sems.at[i]))
+        reads[i].start()
+    for read, write in zip(reads, writes):
+        read.wait()
+        write.start()
+    for write in writes:
+        write.wait()
 
 
 def choose_pieces(sources, source_ids, shifts):
     return pl.pallas_call(
         functools.partial(pieces_kernel, shifts),
         in_specs=[pl.BlockSpec(memory_space=pltpu.SMEM), pl.BlockSpec(memory_space=pl.ANY)],
-        out_specs=[pl.BlockSpec(memory_space=pltpu.VMEM)] * len(shifts),
+        out_specs=[pl.BlockSpec(memory_space=pl.ANY)] * len(shifts),
         out_shape=[jax.ShapeDtypeStruct(sources.shape[1:], sources.dtype)] * len(shifts),
-        scratch_shapes=[pltpu.SemaphoreType.DMA((len(shifts),))],
+        scratch_shapes=[
+            pltpu.VMEM((len(shifts), *sources.shape[1:]), sources.dtype),
+            pltpu.SemaphoreType.DMA((len(shifts),)),
+            pltpu.SemaphoreType.DMA((len(shifts),)),
+        ],
         compiler_params=pltpu.CompilerParams(vmem_limit_bytes=VMEM),
     )(source_ids, sources)
 
@@ -158,17 +167,27 @@
     refs = refs[pieces + 3 :]
     if not first:
         acc_ref, refs = refs[0], refs[1:]
-    out_ref, turned_ref, outer_ref, across_ref = refs[:4]
+    out_ref, turned_ref, outer_ref, across_ref, held_ref, sems = refs[:6]
     a_per = piece_refs[0].shape[0] // extent
     unit_depth = MOST * UNIT_ROWS
     depth = unit_depth * len(units)
     pitch = depth + 8
     step = pl.program_id(0)
 
-    def inner_legs(place, lane, piece_ref):
+    def fetch(piece):
+        return pltpu.make_async_copy(piece_refs[piece], held_ref.at[piece], sems.at[piece])
+
+    @pl.when(step == 0)
+    def fetch_all():
+        for piece in range(pieces):
+            fetch(piece).start()
+
+    def inner_legs(piece):
+        place, lane = piece // per_unit, piece % per_unit
+        fetch(piece).wait()
         sender = (lax.axis_index("work") & (per_unit - 1)) ^ lane
         third = jnp.dot(
-            piece_ref[...], leg3_ref[...], preferred_element_type=jnp.float32
+            held_ref[piece], leg3_ref[...], preferred_element_type=jnp.float32
         ).astype(jnp.bfloat16)
         for d in range(MOST):
             columns = third[:, d * extent : (d + 1) * extent]
@@ -186,13 +205,6 @@
                     :, a * extent : (a + 1) * extent
                 ]
 
-    for piece in range(pieces):
-        pl.when(step == piece)(
-            functools.partial(
-                inner_legs, piece // per_unit, piece % per_unit, piece_refs[piece]
-            )
-        )
-
     @pl.when(step == 0)
     def turn_outer():
         for place, unit in enumerate(units):
@@ -200,6 +212,9 @@
                 unit
             ].astype(jnp.float32)
         across_ref[...] = outer_ref[...].T.astype(jnp.bfloat16)
+
+    for piece in range(pieces):
+        pl.when(step == piece)(functools.partial(inner_legs, piece))
 
     @pl.when(step >= pieces)
     def outer_leg():
@@ -219,12 +234,12 @@
             if not first:
                 part = part + acc_ref[b].astype(jnp.float32)
             if last:
-                refs[4][pl.ds(b, extent, stride=B_BLOCK + 8), :] = part
+                refs[6][pl.ds(b, extent, stride=B_BLOCK + 8), :] = part
             else:
                 out_ref[b] = part.astype(out_ref.dtype)
         if last:
             for a in range(extent):
-                out_ref[a] = refs[4][pl.ds(a * (B_BLOCK + 8), B_BLOCK), :].astype(jnp.bfloat16)
+                out_ref[a] = refs[6][pl.ds(a * (B_BLOCK + 8), B_BLOCK), :].astype(jnp.bfloat16)
 
 
 def add_group(units, pieces, leg3, leg2, leg1, acc, last):
@@ -242,7 +257,8 @@
         return jnp.maximum(i - count, 0)
 
     operands = [*pieces, leg3, leg2, leg1]
-    in_specs = [whole_spec(x) for x in operands]
+    in_specs = [pl.BlockSpec(memory_space=pl.ANY)] * count
+    in_specs += [whole_spec(x) for x in operands[count:]]
     if not first:
         operands.append(acc)
         in_specs.append(pl.BlockSpec((B_BLOCK, extent, extent), lambda i: (block_of(i), 0, 0)))
@@ -250,6 +266,8 @@
         pltpu.VMEM((extent * (depth + 8), extent), jnp.float32),
         pltpu.VMEM((depth, extent), jnp.float32),
         pltpu.VMEM((extent, depth), jnp.bfloat16),
+        pltpu.VMEM((count, *pieces[0].shape), jnp.bfloat16),
+        pltpu.SemaphoreType.DMA((count,)),
     ]
     if last:
         out_shape = jax.ShapeDtypeStruct((extent, extent, extent), jnp.bfloat16)
@@ -303,7 +321,8 @@
     matrices = lax.all_to_all(matrices, "work", split_axis=0, concat_axis=0, tiled=True)
     leg3, leg2, leg1 = make_legs(matrices, sink_counts, weights, workers)
     for place in range(NEAR_AHEAD, len(near)):
-        send(near[place], near[place - NEAR_AHEAD])
+        joined = far[max(place - FAR_AHEAD, 0) : place - FAR_AHEAD + 1] if place < 2 * FAR_AHEAD else []
+        send(near[place], near[place - NEAR_AHEAD], *joined)
 
     acc = None
     sent = FAR_AHEAD

time: 141 us -> 147 us (1.043)
  local copies, waits for them, and re-layouts: 2.75 us -> 15.3 us
  Pallas kernels: 48.9 us -> 36.9 us
  waiting for transfers between devices: 56.6 us -> 62.6 us
    unnamed x40 -> x46, local copies, waits for them, and re-layouts: 2.75 us -> 15.3 us
    pallas_call x3, Pallas kernels: 36.1 us -> 29.5 us  [add_group(): pl.pallas_call(functools.partial(group_kernel, first, last, units, per_un...]
    ppermute x15, waiting for transfers between devices: 56.6 us -> 62.6 us  [send(): lax.ppermute(piece, 'work', [(i, i ^ shift) for i in range(workers)])]
    pallas_call x2, Pallas kernels: 7.17 us -> 3.52 us  [choose_pieces(): pl.pallas_call(functools.partial(pieces_kernel, shifts), in_specs=[pl.Blo...]
  transfers between devices with their start and end apart: 16 -> 16, of which waited for: 7 -> 9; matrix products, arithmetic and copies ran while one was open for 0% -> 0% of each run, Pallas kernels for 27% -> 20%
where the time goes in v3:
time: 147 us
  waiting for transfers between devices  62.6 us (43%)
  Pallas kernels  36.9 us (25%)
  starting transfers between devices  31.6 us (21%)
  local copies, waits for them, and re-layouts  15.3 us (10%)
    ppermute x15, waiting for transfers between devices, send(): lax.ppermute(piece, 'work', [(i, i ^ shift) for i in range(workers)])  62.6 us
    pallas_call x3, Pallas kernels, add_group(): pl.pallas_call(functools.partial(group_kernel, first, last, units, per_un...  29.5 us
    ppermute x15, starting transfers between devices, send(): lax.ppermute(piece, 'work', [(i, i ^ shift) for i in range(workers)])  25.6 us
    unnamed x46, local copies, waits for them, and re-layouts  15.3 us
    all_to_all x1, starting transfers between devices, per_device(): lax.all_to_all(matrices, 'work', split_axis=0, concat_axis=0, tiled=True)  6.07 us
    pallas_call x2, Pallas kernels, choose_pieces(): pl.pallas_call(functools.partial(pieces_kernel, shifts), in_specs=[pl.Blo...  3.52 us
  transfers between devices with their start and end apart: 16, of which 9 were waited for; matrix products, arithmetic and copies ran while one was open for 0% of the time, Pallas kernels for 20%

profile of v3, /device:TPU:11, one launch (start us, length us, event | category | flops | bytes accessed | tf_op | source)
XLA Modules:
  0.0 146.8 jit_solution(17810431396328801152)
XLA Ops:
  0.0 2.2 %copy-done = bf16[16,1024,128]{2,1,0:T(8,128)(2,1)S(1)} copy-done((bf16[16,1024,128]{2,1,0:T(8,128)(2,1)S(1)}, bf16[16,1024,128]{2,1,0:T(8,128)(2,1)}, u32[]{:S(2)}) %copy-start) | copy-done | bytes 4194328
  2.9 1.6 %shard_map.65 = (bf16[1024,128]{1,0:T(8,128)(2,1)}, bf16[1024,128]{1,0:T(8,128)(2,1)S(1)}, bf16[1024,128]{1,0:T(8,128)(2,1)S(1)}, bf16[1024,128]{1,0:T(8,128)(2,1)S(1)}, bf16[1024,128]{1,0:T(8,128)(2,1)}) custom-call(s32[16]{0:T(128)S(1)} %copy-done.5, bf16[16,1024,128]{2,1,0:T(8,128)(2,1)S(1)} %copy-done), custom_call_target="tpu_custom_call" | custom-call | tf_op jit(solution)/shard_map/pallas_call | solution.py:41
  5.2 2.2 %shard_map.66 = bf16[16,144,128]{2,1,0:T(8,128)(2,1)} custom-call(s32[16]{0:T(128)S(1)} %copy-done.7, s32[3,48]{1,0:T(4,128)S(1)} %bitcast.2, bf16[96,1024]{1,0:T(8,128)(2,1)S(1)} %copy-done.3), custom_call_target="tpu_custom_call" | custom-call | tf_op jit(solution)/shard_map/pallas_call | solution.py:88
  7.4 6.1 %all-to-all-start = ((bf16[16,144,128]{2,1,0:T(8,128)(2,1)}), bf16[16,144,128]{2,1,0:T(8,128)(2,1)S(1)}, u32[]{:S(2)}, u32[]{:S(2)}) async-start(bf16[16,144,128]{2,1,0:T(8,128)(2,1)} %shard_map.66), calls=%async_computation | async-start | bytes 1179648 | tf_op jit(solution)/shard_map/all_to_all | solution.py:321
  13.6 2.3 %collective-permute-start.1 = (bf16[1024,128]{1,0:T(8,128)(2,1)}, bf16[1024,128]{1,0:T(8,128)(2,1)S(1)}, u32[]{:S(2)}, u32[]{:S(2)}) collective-permute-start(bf16[1024,128]{1,0:T(8,128)(2,1)} %get-tuple-element.59), channel_id=1, source_target_pairs={{0,8},{1,9},{2,10},{3,11},{4,12},{5,13},{6,14},{7,15},{8,0},{9,1},... | collective-permute-start | bytes 786440 | tf_op jit(solution)/shard_map/ppermute | solution.py:315
  15.9 2.2 %copy-done.1 = bf16[16,1024,128]{2,1,0:T(8,128)(2,1)S(1)} copy-done((bf16[16,1024,128]{2,1,0:T(8,128)(2,1)S(1)}, bf16[16,1024,128]{2,1,0:T(8,128)(2,1)}, u32[]{:S(2)}) %copy-start.1) | copy-done | bytes 4194328
  18.1 1.9 %shard_map.64 = (bf16[1024,128]{1,0:T(8,128)(2,1)S(1)}, bf16[1024,128]{1,0:T(8,128)(2,1)S(1)}, bf16[1024,128]{1,0:T(8,128)(2,1)S(1)}, bf16[1024,128]{1,0:T(8,128...) custom-call(s32[16]{0:T(128)S(1)} %copy-done.6, ...), custom_call_target="tpu_custom_call" | custom-call | tf_op jit(solution)/shard_map/pallas_call | solution.py:41
  20.7 2.0 %collective-permute-start.5 = (bf16[1024,128]{1,0:T(8,128)(2,1)S(1)}, bf16[1024,128]{1,0:T(8,128)(2,1)S(1)}, u32[]{:S(2)}, u32[]{:S(2)}) collective-permute-start(bf16[1024,128]{1,0:T(8,128)(2,1)S(1)} %get-tuple-element.69), channel_id=1, source_target_pairs={{0,5},{1,4},{2,7},{3,6},{4,1},{5,0},{6,3},{7,2},{8,13},{9,12},{10,... | collective-permute-start | bytes 786440 | tf_op jit(solution)/shard_map/ppermute | solution.py:315
  22.7 2.7 %collective-permute-start.10 = (bf16[1024,128]{1,0:T(8,128)(2,1)S(1)}, bf16[1024,128]{1,0:T(8,128)(2,1)S(1)}, u32[]{:S(2)}, u32[]{:S(2)}) collective-permute-start(bf16[1024,128]{1,0:T(8,128)(2,1)S(1)} %copy-done.16), channel_id=1, source_target_pairs={{0,10},{1,11},{2,8},{3,9},{4,14},{5,15},{6,12},{7,13},{8,2},{9,3},... | collective-permute-start | bytes 786440 | tf_op jit(solution)/shard_map/ppermute | solution.py:315
  25.5 6.8 %collective-permute-done.refs_4_ = bf16[1024,128]{1,0:T(8,128)(2,1)S(1)} collective-permute-done((bf16[1024,128]{1,0:T(8,128)(2,1)}, bf16[1024,128]{1,0:T(8,128)(2,1)S(1)}, u32[]{:S(2)}, u32[]{:S(2)}) %collective-permute-start) | collective-permute-done | bytes 262176 | tf_op jit(solution)/shard_map/ppermute | solution.py:315
  32.3 5.6 %collective-permute-done.1.refs_8_ = bf16[1024,128]{1,0:T(8,128)(2,1)S(1)} collective-permute-done((bf16[1024,128]{1,0:T(8,128)(2,1)}, bf16[1024,128]{1,0:T(8,128)(2,1)S(1)}, u32[]{:S(2)}, u32[]{:S(2)}) %collective-permute-start.1) | collective-permute-done | bytes 262176 | tf_op jit(solution)/shard_map/ppermute | solution.py:315
  37.9 3.9 %collective-permute-start.9 = (bf16[1024,128]{1,0:T(8,128)(2,1)S(1)}, bf16[1024,128]{1,0:T(8,128)(2,1)S(1)}, u32[]{:S(2)}, u32[]{:S(2)}) collective-permute-start(bf16[1024,128]{1,0:T(8,128)(2,1)S(1)} %get-tuple-element.83), channel_id=1, source_target_pairs={{0,6},{1,7},{2,4},{3,5},{4,2},{5,3},{6,0},{7,1},{8,14},{9,15},{10,... | collective-permute-start | bytes 786440 | tf_op jit(solution)/shard_map/ppermute | solution.py:315
  41.8 1.6 %collective-permute-done.5.refs_5_ = bf16[1024,128]{1,0:T(8,128)(2,1)S(1)} collective-permute-done((bf16[1024,128]{1,0:T(8,128)(2,1)S(1)}, bf16[1024,128]{1,0:T(8,128)(2,1)S(1)}, u32[]{:S(2)}, u32[]{:S(2)}) %collective-permute-start.5) | collective-permute-done | bytes 262176 | tf_op jit(solution)/shard_map/ppermute | solution.py:315
  44.1 10.5 %collective-permute-done.6.refs_9_ = bf16[1024,128]{1,0:T(8,128)(2,1)S(1)} collective-permute-done((bf16[1024,128]{1,0:T(8,128)(2,1)S(1)}, bf16[1024,128]{1,0:T(8,128)(2,1)S(1)}, u32[]{:S(2)}, u32[]{:S(2)}) %collective-permute-start.6) | collective-permute-done | bytes 262176 | tf_op jit(solution)/shard_map/ppermute | solution.py:315
  55.3 4.3 %collective-permute-start.12 = (bf16[1024,128]{1,0:T(8,128)(2,1)S(1)}, bf16[1024,128]{1,0:T(8,128)(2,1)S(1)}, u32[]{:S(2)}, u32[]{:S(2)}) collective-permute-start(bf16[1024,128]{1,0:T(8,128)(2,1)S(1)} %get-tuple-element.88), channel_id=1, source_target_pairs={{0,7},{1,6},{2,5},{3,4},{4,3},{5,2},{6,1},{7,0},{8,15},{9,14},{10,... | collective-permute-start | bytes 786440 | tf_op jit(solution)/shard_map/ppermute | solution.py:315
  59.6 1.2 collective-permute-done.9.refs_6_
  62.1 5.0 %collective-permute-done.12.refs_7_ = bf16[1024,128]{1,0:T(8,128)(2,1)S(1)} collective-permute-done((bf16[1024,128]{1,0:T(8,128)(2,1)S(1)}, bf16[1024,128]{1,0:T(8,128)(2,1)S(1)}, u32[]{:S(2)}, u32[]{:S(2)}) %collective-permute-start.12) | collective-permute-done | bytes 262176 | tf_op jit(solution)/shard_map/ppermute | solution.py:315
  67.9 1.6 %collective-permute-start.13 = (bf16[1024,128]{1,0:T(8,128)(2,1)}, bf16[1024,128]{1,0:T(8,128)(2,1)}, u32[]{:S(2)}, u32[]{:S(2)}) collective-permute-start(bf16[1024,128]{1,0:T(8,128)(2,1)} %get-tuple-element.89), channel_id=1, source_target_pairs={{0,3},{1,2},{2,1},{3,0},{4,7},{5,6},{6,5},{7,4},{8,11},{9,10},{10,... | collective-permute-start | bytes 786440 | tf_op jit(solution)/shard_map/ppermute | solution.py:315
  69.5 2.9 %collective-permute-start.2 = (bf16[1024,128]{1,0:T(8,128)(2,1)S(1)}, bf16[1024,128]{1,0:T(8,128)(2,1)S(1)}, u32[]{:S(2)}, u32[]{:S(2)}) collective-permute-start(bf16[1024,128]{1,0:T(8,128)(2,1)S(1)} %get-tuple-element.61), channel_id=1, source_target_pairs={{0,11},{1,10},{2,9},{3,8},{4,15},{5,14},{6,13},{7,12},{8,3},{9,2},... | collective-permute-start | bytes 786440 | tf_op jit(solution)/shard_map/ppermute | solution.py:315
  72.3 1.3 collective-permute-start.7
  73.7 1.7 %shard_map.67 = (bf16[128,768]{1,0:T(8,128)(2,1)S(1)}, bf16[768,128]{1,0:T(8,128)(2,1)S(1)}, bf16[8,96,128]{2,1,0:T(8,128)(2,1)S(1)}) custom-call(s32[16]{0:T(128)S(1)} %copy-done.7, f32[48]{0:T(128)S(1)} %copy-done.8, bf16[16,144,128]{2,1,0:T(8,128)(2,1)S(1)} %all-to-all-done.matrix_ref), custom_call_target="tpu_custom_call" | custom-call | tf_op jit(solution)/shard_map/pallas_call | solution.py:144
  75.4 8.5 %collective-permute-done.13.refs_3_ = bf16[1024,128]{1,0:T(8,128)(2,1)} collective-permute-done((bf16[1024,128]{1,0:T(8,128)(2,1)}, bf16[1024,128]{1,0:T(8,128)(2,1)}, u32[]{:S(2)}, u32[]{:S(2)}) %collective-permute-start.13) | collective-permute-done | bytes 262176 | tf_op jit(solution)/shard_map/ppermute | solution.py:315
  83.9 0.9 copy-done.10
  85.8 0.9 copy-done.14
  88.6 14.7 %shard_map.68.refs_7_ = bf16[128,128,128]{2,1,0:T(8,128)(2,1)S(1)} custom-call(bf16[1024,128]{1,0:T(8,128)(2,1)S(1)} %copy-done.10, bf16[1024,128]{1,0:T(8,128)(2,1)S(1)} %collective-permute-done.4.refs_1_, bf16[1024,128]{1,0:T(8,128)(2,1)} %collective-permute-done.11.refs_2_, bf16[1024,128]{1,0:T(8,128)(2,1)} %collective-permute-done.13.refs_3_, ...), custom_call_target="tpu_custom_call" | custom-call | flops 6039797760 | bytes 25165824 | tf_op jit(solution)/shard_map/pallas_call | solution.py:280
  103.3 2.0 %copy-done.2 = bf16[128,128,128]{2,1,0:T(8,128)(2,1)} copy-done((bf16[128,128,128]{2,1,0:T(8,128)(2,1)}, bf16[128,128,128]{2,1,0:T(8,128)(2,1)S(1)}, u32[]{:S(2)}) %copy-start.2) | copy-done | bytes 4194328
  105.8 1.2 collective-permute-start.3
  107.1 1.4 collective-permute-start.8
  108.5 20.8 %collective-permute-done.14.refs_3_ = bf16[1024,128]{1,0:T(8,128)(2,1)S(1)} collective-permute-done((bf16[1024,128]{1,0:T(8,128)(2,1)S(1)}, bf16[1024,128]{1,0:T(8,128)(2,1)S(1)}, u32[]{:S(2)}, u32[]{:S(2)}) %collective-permute-start.14) | collective-permute-done | bytes 262176 | tf_op jit(solution)/shard_map/ppermute | solution.py:315
  129.3 8.6 %shard_map.69.refs_5_ = bf16[128,128,128]{2,1,0:T(8,128)(2,1)S(1)} custom-call(bf16[1024,128]{1,0:T(8,128)(2,1)S(1)} %collective-permute-done.10.refs_0_, bf16[1024,128]{1,0:T(8,128)(2,1)S(1)} %collective-permute-done.2.refs_1_, bf16[1024,128]{1,0:T(8,128)(2,1)S(1)} %collective-permute-done.7.refs_2_, bf16[1024,128]{1,0:T(8,128)(2,1)S(1)} %collective-permute-done.14.refs_3_, ...), custom_call_target="tpu_custom_call" | custom-call | flops 2415919104 | bytes 25165824 | tf_op jit(solution)/shard_map/pallas_call | solution.py:280
  137.9 2.5 %collective-permute-done.8.refs_1_ = bf16[1024,128]{1,0:T(8,128)(2,1)S(1)} collective-permute-done((bf16[1024,128]{1,0:T(8,128)(2,1)S(1)}, bf16[1024,128]{1,0:T(8,128)(2,1)S(1)}, u32[]{:S(2)}, u32[]{:S(2)}) %collective-permute-start.8) | collective-permute-done | bytes 262176 | tf_op jit(solution)/shard_map/ppermute | solution.py:315
  140.4 6.2 %shard_map.70 = bf16[128,128,128]{2,1,0:T(8,128)(2,1)} custom-call(bf16[1024,128]{1,0:T(8,128)(2,1)S(1)} %collective-permute-done.3.refs_0_, bf16[1024,128]{1,0:T(8,128)(2,1)S(1)} %collective-permute-done.8.refs_1_, bf16[128,768]{1,0:T(8,128)(2,1)S(1)} %get-tuple-element.76.refs_10_.refs_4_.refs_2_, ...), custom_call_target="tpu_custom_call" | custom-call | flops 1207959552 | bytes 25165824 | tf_op jit(solution)/shard_map/pallas_call | solution.py:280
  (53 shorter events, 9.0 us)
Async XLA Ops:
  0.0 2.2 %copy-start = (bf16[16,1024,128]{2,1,0:T(8,128)(2,1)S(1)}, bf16[16,1024,128]{2,1,0:T(8,128)(2,1)}, u32[]{:S(2)}) copy-start(bf16[16,1024,128]{2,1,0:T(8,128)(2,1)} %source_ref.3) | copy-start | bytes 12582916
  2.8 2.4 %copy-start.3 = (bf16[96,1024]{1,0:T(8,128)(2,1)S(1)}, bf16[96,1024]{1,0:T(8,128)(2,1)}, u32[]{:S(2)}) copy-start(bf16[96,1024]{1,0:T(8,128)(2,1)} %peramb_ref.1) | copy-start | bytes 589828
  2.8 2.4 %copy-start.4 = (s32[48,3]{0,1:T(4,128)S(1)}, s32[48,3]{0,1:T(4,128)}, u32[]{:S(2)}) copy-start(s32[48,3]{0,1:T(4,128)} %param.9) | copy-start | bytes 1732
  2.8 2.4 %copy-start.7 = (s32[16]{0:T(128)S(1)}, s32[16]{0:T(128)}, u32[]{:S(2)}) copy-start(s32[16]{0:T(128)} %counts_ref.3) | copy-start | bytes 196
  2.9 13.0 %copy-start.6 = (s32[16]{0:T(128)S(1)}, s32[16]{0:T(128)}, u32[]{:S(2)}) copy-start(s32[16]{0:T(128)} %ids_ref.3) | copy-start | bytes 196
  2.9 70.8 %copy-start.8 = (f32[48]{0:T(128)S(1)}, f32[48]{0:T(128)}, u32[]{:S(2)}) copy-start(f32[48]{0:T(128)} %weights_ref.1) | copy-start | bytes 580
  4.4 3.0 %copy-start.15 = (bf16[1024,128]{1,0:T(8,128)(2,1)}, bf16[1024,128]{1,0:T(8,128)(2,1)S(1)}, u32[]{:S(2)}) copy-start(bf16[1024,128]{1,0:T(8,128)(2,1)S(1)} %get-tuple-element.85) | copy-start | bytes 786436
  4.5 3.0 %copy-start.19 = (bf16[1024,128]{1,0:T(8,128)(2,1)}, bf16[1024,128]{1,0:T(8,128)(2,1)S(1)}, u32[]{:S(2)}) copy-start(bf16[1024,128]{1,0:T(8,128)(2,1)S(1)} %get-tuple-element.71) | copy-start | bytes 786436
  4.5 3.0 %collective-permute-start.4 = (bf16[1024,128]{1,0:T(8,128)(2,1)S(1)}, bf16[1024,128]{1,0:T(8,128)(2,1)S(1)}, u32[]{:S(2)}, u32[]{:S(2)}) collective-permute-start(bf16[1024,128]{1,0:T(8,128)(2,1)S(1)} %get-tuple-element.67), channel_id=1, source_target_pairs={{0,1},{1,0},{2,3},{3,2},{4,5},{5,4},{6,7},{7,6},{8,9},{9,8},{10,11... | collective-permute-start | bytes 786440 | tf_op jit(solution)/shard_map/ppermute | solution.py:315
  7.4 66.2 %all-to-all-start = ((bf16[16,144,128]{2,1,0:T(8,128)(2,1)}), bf16[16,144,128]{2,1,0:T(8,128)(2,1)S(1)}, u32[]{:S(2)}, u32[]{:S(2)}) async-start(bf16[16,144,128]{2,1,0:T(8,128)(2,1)} %shard_map.66), calls=%async_computation | async-start | bytes 1179648 | tf_op jit(solution)/shard_map/all_to_all | solution.py:321
  13.5 18.8 %collective-permute-start = (bf16[1024,128]{1,0:T(8,128)(2,1)}, bf16[1024,128]{1,0:T(8,128)(2,1)S(1)}, u32[]{:S(2)}, u32[]{:S(2)}) collective-permute-start(bf16[1024,128]{1,0:T(8,128)(2,1)} %get-tuple-element.57), channel_id=1, source_target_pairs={{0,4},{1,5},{2,6},{3,7},{4,0},{5,1},{6,2},{7,3},{8,12},{9,13},{10,... | collective-permute-start | bytes 786440 | tf_op jit(solution)/shard_map/ppermute | solution.py:315
  13.6 24.3 %collective-permute-start.1 = (bf16[1024,128]{1,0:T(8,128)(2,1)}, bf16[1024,128]{1,0:T(8,128)(2,1)S(1)}, u32[]{:S(2)}, u32[]{:S(2)}) collective-permute-start(bf16[1024,128]{1,0:T(8,128)(2,1)} %get-tuple-element.59), channel_id=1, source_target_pairs={{0,8},{1,9},{2,10},{3,11},{4,12},{5,13},{6,14},{7,15},{8,0},{9,1},... | collective-permute-start | bytes 786440 | tf_op jit(solution)/shard_map/ppermute | solution.py:315
  15.9 2.2 %copy-start.1 = (bf16[16,1024,128]{2,1,0:T(8,128)(2,1)S(1)}, bf16[16,1024,128]{2,1,0:T(8,128)(2,1)}, u32[]{:S(2)}) copy-start(bf16[16,1024,128]{2,1,0:T(8,128)(2,1)} %source_ref.3) | copy-start | bytes 12582916
  18.1 4.7 %copy-start.20 = (bf16[1024,128]{1,0:T(8,128)(2,1)S(1)}, bf16[1024,128]{1,0:T(8,128)(2,1)}, u32[]{:S(2)}) copy-start(bf16[1024,128]{1,0:T(8,128)(2,1)} %copy-done.19) | copy-start | bytes 786436
  18.1 4.7 %copy-start.16 = (bf16[1024,128]{1,0:T(8,128)(2,1)S(1)}, bf16[1024,128]{1,0:T(8,128)(2,1)}, u32[]{:S(2)}) copy-start(bf16[1024,128]{1,0:T(8,128)(2,1)} %copy-done.15) | copy-start | bytes 786436
  20.7 22.7 %collective-permute-start.5 = (bf16[1024,128]{1,0:T(8,128)(2,1)S(1)}, bf16[1024,128]{1,0:T(8,128)(2,1)S(1)}, u32[]{:S(2)}, u32[]{:S(2)}) collective-permute-start(bf16[1024,128]{1,0:T(8,128)(2,1)S(1)} %get-tuple-element.69), channel_id=1, source_target_pairs={{0,5},{1,4},{2,7},{3,6},{4,1},{5,0},{6,3},{7,2},{8,13},{9,12},{10,... | collective-permute-start | bytes 786440 | tf_op jit(solution)/shard_map/ppermute | solution.py:315
  22.7 31.9 %collective-permute-start.6 = (bf16[1024,128]{1,0:T(8,128)(2,1)S(1)}, bf16[1024,128]{1,0:T(8,128)(2,1)S(1)}, u32[]{:S(2)}, u32[]{:S(2)}) collective-permute-start(bf16[1024,128]{1,0:T(8,128)(2,1)S(1)} %copy-done.20), channel_id=1, source_target_pairs={{0,9},{1,8},{2,11},{3,10},{4,13},{5,12},{6,15},{7,14},{8,1},{9,0},... | collective-permute-start | bytes 786440 | tf_op jit(solution)/shard_map/ppermute | solution.py:315
  22.7 38.8 %collective-permute-start.10 = (bf16[1024,128]{1,0:T(8,128)(2,1)S(1)}, bf16[1024,128]{1,0:T(8,128)(2,1)S(1)}, u32[]{:S(2)}, u32[]{:S(2)}) collective-permute-start(bf16[1024,128]{1,0:T(8,128)(2,1)S(1)} %copy-done.16), channel_id=1, source_target_pairs={{0,10},{1,11},{2,8},{3,9},{4,14},{5,15},{6,12},{7,13},{8,2},{9,3},... | collective-permute-start | bytes 786440 | tf_op jit(solution)/shard_map/ppermute | solution.py:315
  37.9 23.0 %collective-permute-start.9 = (bf16[1024,128]{1,0:T(8,128)(2,1)S(1)}, bf16[1024,128]{1,0:T(8,128)(2,1)S(1)}, u32[]{:S(2)}, u32[]{:S(2)}) collective-permute-start(bf16[1024,128]{1,0:T(8,128)(2,1)S(1)} %get-tuple-element.83), channel_id=1, source_target_pairs={{0,6},{1,7},{2,4},{3,5},{4,2},{5,3},{6,0},{7,1},{8,14},{9,15},{10,... | collective-permute-start | bytes 786440 | tf_op jit(solution)/shard_map/ppermute | solution.py:315
  55.3 11.8 %collective-permute-start.12 = (bf16[1024,128]{1,0:T(8,128)(2,1)S(1)}, bf16[1024,128]{1,0:T(8,128)(2,1)S(1)}, u32[]{:S(2)}, u32[]{:S(2)}) collective-permute-start(bf16[1024,128]{1,0:T(8,128)(2,1)S(1)} %get-tuple-element.88), channel_id=1, source_target_pairs={{0,7},{1,6},{2,5},{3,4},{4,3},{5,2},{6,1},{7,0},{8,15},{9,14},{10,... | collective-permute-start | bytes 786440 | tf_op jit(solution)/shard_map/ppermute | solution.py:315
  61.6 13.8 %collective-permute-start.11 = (bf16[1024,128]{1,0:T(8,128)(2,1)}, bf16[1024,128]{1,0:T(8,128)(2,1)}, u32[]{:S(2)}, u32[]{:S(2)}) collective-permute-start(bf16[1024,128]{1,0:T(8,128)(2,1)} %get-tuple-element.86), channel_id=1, source_target_pairs={{0,2},{1,3},{2,0},{3,1},{4,6},{5,7},{6,4},{7,5},{8,10},{9,11},{10,... | collective-permute-start | bytes 786440 | tf_op jit(solution)/shard_map/ppermute | solution.py:315
  67.9 16.0 %collective-permute-start.13 = (bf16[1024,128]{1,0:T(8,128)(2,1)}, bf16[1024,128]{1,0:T(8,128)(2,1)}, u32[]{:S(2)}, u32[]{:S(2)}) collective-permute-start(bf16[1024,128]{1,0:T(8,128)(2,1)} %get-tuple-element.89), channel_id=1, source_target_pairs={{0,3},{1,2},{2,1},{3,0},{4,7},{5,6},{6,5},{7,4},{8,11},{9,10},{10,... | collective-permute-start | bytes 786440 | tf_op jit(solution)/shard_map/ppermute | solution.py:315
  69.5 36.4 %collective-permute-start.2 = (bf16[1024,128]{1,0:T(8,128)(2,1)S(1)}, bf16[1024,128]{1,0:T(8,128)(2,1)S(1)}, u32[]{:S(2)}, u32[]{:S(2)}) collective-permute-start(bf16[1024,128]{1,0:T(8,128)(2,1)S(1)} %get-tuple-element.61), channel_id=1, source_target_pairs={{0,11},{1,10},{2,9},{3,8},{4,15},{5,14},{6,13},{7,12},{8,3},{9,2},... | collective-permute-start | bytes 786440 | tf_op jit(solution)/shard_map/ppermute | solution.py:315
  72.3 34.7 %collective-permute-start.7 = (bf16[1024,128]{1,0:T(8,128)(2,1)S(1)}, bf16[1024,128]{1,0:T(8,128)(2,1)S(1)}, u32[]{:S(2)}, u32[]{:S(2)}) collective-permute-start(bf16[1024,128]{1,0:T(8,128)(2,1)S(1)} %get-tuple-element.73), channel_id=1, source_target_pairs={{0,12},{1,13},{2,14},{3,15},{4,8},{5,9},{6,10},{7,11},{8,4},{9,5},... | collective-permute-start | bytes 786440 | tf_op jit(solution)/shard_map/ppermute | solution.py:315
  83.9 1.0 copy-start.10
  84.8 0.9 copy-start.12
  85.8 0.9 copy-start.14
  86.7 0.9 copy-start.18
  103.3 2.0 %copy-start.2 = (bf16[128,128,128]{2,1,0:T(8,128)(2,1)}, bf16[128,128,128]{2,1,0:T(8,128)(2,1)S(1)}, u32[]{:S(2)}) copy-start(bf16[128,128,128]{2,1,0:T(8,128)(2,1)S(1)} %shard_map.68.refs_7_) | copy-start | bytes 12582916
  105.3 24.0 %collective-permute-start.14 = (bf16[1024,128]{1,0:T(8,128)(2,1)S(1)}, bf16[1024,128]{1,0:T(8,128)(2,1)S(1)}, u32[]{:S(2)}, u32[]{:S(2)}) collective-permute-start(bf16[1024,128]{1,0:T(8,128)(2,1)S(1)} %get-tuple-element.101), channel_id=1, source_target_pairs={{0,13},{1,12},{2,15},{3,14},{4,9},{5,8},{6,11},{7,10},{8,5},{9,4},... | collective-permute-start | bytes 786440 | tf_op jit(solution)/shard_map/ppermute | solution.py:315
  105.8 32.1 %collective-permute-start.3 = (bf16[1024,128]{1,0:T(8,128)(2,1)S(1)}, bf16[1024,128]{1,0:T(8,128)(2,1)S(1)}, u32[]{:S(2)}, u32[]{:S(2)}) collective-permute-start(bf16[1024,128]{1,0:T(8,128)(2,1)S(1)} %get-tuple-element.62), channel_id=1, source_target_pairs={{0,14},{1,15},{2,12},{3,13},{4,10},{5,11},{6,8},{7,9},{8,6},{9,7},... | collective-permute-start | bytes 786440 | tf_op jit(solution)/shard_map/ppermute | solution.py:315
  107.1 33.3 %collective-permute-start.8 = (bf16[1024,128]{1,0:T(8,128)(2,1)S(1)}, bf16[1024,128]{1,0:T(8,128)(2,1)S(1)}, u32[]{:S(2)}, u32[]{:S(2)}) collective-permute-start(bf16[1024,128]{1,0:T(8,128)(2,1)S(1)} %get-tuple-element.74), channel_id=1, source_target_pairs={{0,15},{1,14},{2,13},{3,12},{4,11},{5,10},{6,9},{7,8},{8,7},{9,6},... | collective-permute-start | bytes 786440 | tf_op jit(solution)/shard_map/ppermute | solution.py:315
  (7 other events, 5.1 us)
